TPU v7x, 256 devices: a whole 4x4x8 slice. The times are simulated.
256 devices in a mesh: blk: 64 (over z, x, y_lo), probe: 4 (over y_hi, core).
Axes of the slice: x: 4, y: 4 (y_hi: 2, y_lo: 2; y = y_hi * 2 + y_lo), z: 8, core: 2. Of those that a mesh axis runs over, the one named last changes fastest.
Arguments:
- points: float32 [8, 40960], P(None, ('blk', 'probe')), may hold values from -6 to 6
- targets: float32 [40960], P('blk'), may hold values from -12 to 12
- signs: int32 [15, 40960], P(None, 'blk'), may hold values from 0 to 1
Outputs:
- solution: float32 [16, 40960], P('probe', 'blk')
- residual: float32 [16, 40960], P('probe', 'blk')
- direction: float32 [16, 40960], P('probe', 'blk')
- coeffs: float32 [2, 2, 16], P(None, None, 'probe')
All inputs are finite; a program needn't handle non-finite values.
Results may differ from a plain program's by a relative error of at most 0.005.
Values may be sent and summed in bfloat16 or wider, within the bound.
No kernel may reach another device: no remote copies, remote signals or barrier semaphores. Data moves between devices by JAX's collectives and lax.ppermute only.
A program may use at most 64 MiB of HBM per device.

v0:
```python
import math

import jax
import jax.numpy as jnp
from jax import lax
from jax.sharding import PartitionSpec as P

COLS = 16
ITERS = 2


def kernel_product(own_points, other_points, direction):
    cross = lax.dot_general(
        other_points,
        own_points,
        (((0,), (0,)), ((), ())),
        precision=lax.Precision.HIGHEST,
        preferred_element_type=jnp.float32,
    )
    norm_other = jnp.sum(other_points * other_points, 0)
    norm_own = jnp.sum(own_points * own_points, 0)
    squared = norm_other[:, None] + norm_own[None, :] - 2.0 * cross
    tile = jnp.exp(-0.5 * squared).astype(jnp.bfloat16)
    return jnp.dot(direction, tile, preferred_element_type=jnp.float32)


def fold_rows(running, own_points, other_points, direction):
    width = other_points.shape[1]
    block_rows = math.gcd(width, 1024)
    block_count = width // block_rows

    def one_block(block, acc):
        offset = block * block_rows
        part_points = lax.dynamic_slice_in_dim(other_points, offset, block_rows, 1)
        part_dir = lax.dynamic_slice_in_dim(direction, offset, block_rows, 1)
        return acc + kernel_product(own_points, part_points, part_dir)

    return lax.fori_loop(0, block_count, one_block, running)


def start_total(values):
    return lax.psum(values, "blk")


def curv_total(values):
    return lax.psum(values, "blk")


def norm_total(values):
    return lax.psum(values, "blk")


def on_device(points, targets, signs):
    probe_count = lax.axis_size("probe")
    block_count = targets.shape[0]
    rhs_all = jnp.concatenate([targets[None, :], 2.0 * signs.astype(jnp.float32) - 1.0], 0)
    col_count = COLS // probe_count
    rhs = lax.dynamic_slice_in_dim(rhs_all, lax.axis_index("probe") * col_count, col_count, 0)
    empty = jnp.zeros((col_count, block_count), jnp.float32)
    own_points = lax.all_gather(points, "probe", axis=1, tiled=True)
    solution = jnp.zeros_like(rhs)
    residual = rhs
    direction = rhs
    norm_now = start_total(jnp.sum(residual * residual, 1))
    step_list = []
    ratio_list = []
    for iteration in range(ITERS):
        kernel_image = (
            fold_rows(
                empty,
                own_points,
                lax.all_gather(own_points, "blk", axis=1, tiled=True),
                lax.all_gather(
                    direction.astype(jnp.bfloat16).astype(jnp.float32), "blk", axis=1, tiled=True
                ).astype(jnp.bfloat16),
            )
            + 0.5 * direction
        )
        curvature = curv_total(jnp.sum(direction * kernel_image, 1))
        step_size = norm_now / curvature
        solution = solution + step_size[:, None] * direction
        residual = residual - step_size[:, None] * kernel_image
        norm_next = norm_total(jnp.sum(residual * residual, 1))
        dir_ratio = norm_next / norm_now
        direction = residual + dir_ratio[:, None] * direction
        norm_now = norm_next
        step_list.append(step_size)
        ratio_list.append(dir_ratio)
    coeffs = jnp.stack([jnp.stack(step_list), jnp.stack(ratio_list)])
    return (solution, residual, direction, coeffs)


def solution(mesh):
    placed = (P(None, ("blk", "probe")), P("blk"), P(None, "blk"))
    return jax.shard_map(
        on_device,
        mesh=mesh,
        in_specs=placed,
        out_specs=(P("probe", "blk"), P("probe", "blk"), P("probe", "blk"), P(None, None, "probe")),
        check_vma=False,
    )
```

profile of v0, /device:TPU:16, one launch (start us, length us, event | category | flops | bytes accessed | tf_op | source)
XLA Modules:
  0.0 1459.5 jit_solution(11944136815164497503)
XLA Ops:
  7.2 6.9 all-gather
  17.1 160.4 %all_gather.13 = bf16[4,40960]{1,0:T(4,128)(2,1)S(1)} all-gather(bf16[4,640]{1,0:T(4,128)(2,1)S(1)} %get-tuple-element.346), channel_id=1, replica_groups=mesh['blk'=64,'probe'=4] {'blk'}, dimensions={1}, use_global_device_ids=true | all-gather | bytes 332800 | tf_op jit(solution)/shard_map/all_gather | solution.py:73
  177.5 138.3 %all-gather.3.cloned.1.call-done = f32[8,40960]{1,0:T(8,128)} async-done(((f32[8,640]{1,0:T(8,128)}), f32[8,40960]{1,0:T(8,128)}) %all-gather.3.cloned.1.call-update) | async-done | bytes 1310736 | tf_op jit(solution)/shard_map/all_gather | solution.py:72
  315.8 182.2 %while.32 = (s32[]{:T(128)}, f32[4,640]{1,0:T(4,128)S(1)}, bf16[4,40960]{1,0:T(4,128)(2,1)S(1)}, f32[8,40960]{1,0:T(8,128)}, f32[640]{0:T(1024)S(1)}, /*index=5*...) while((s32[]{:T(128)}, f32[4,640]{1,0:T(4,128)S(1)}, ...), condition=%wide.region_5.0_spmd.clone, body=%wide.region_3.5_spmd.clone.sunk | while | flops 71454720 | bytes 2747057 | solution.py:38
  316.6 3.5 exponential_convert_fusion.4
  330.2 3.5 exponential_convert_fusion.4
  339.3 3.5 exponential_convert_fusion.4
  348.5 3.5 exponential_convert_fusion.4
  357.6 3.5 exponential_convert_fusion.4
  366.7 3.5 exponential_convert_fusion.4
  375.8 3.5 exponential_convert_fusion.4
  384.9 3.5 exponential_convert_fusion.4
  394.0 3.5 exponential_convert_fusion.4
  403.1 3.5 exponential_convert_fusion.4
  412.2 3.5 exponential_convert_fusion.4
  421.3 3.5 exponential_convert_fusion.4
  430.5 3.5 exponential_convert_fusion.4
  439.6 3.5 exponential_convert_fusion.4
  448.7 3.5 exponential_convert_fusion.4
  457.8 3.5 exponential_convert_fusion.4
  466.9 3.5 exponential_convert_fusion.4
  476.0 3.5 exponential_convert_fusion.4
  485.1 3.5 exponential_convert_fusion.4
  494.2 3.5 exponential_convert_fusion.4
  498.2 157.2 %all-reduce = (f32[4]{0:T(128)S(1)}, f32[4]{0:T(128)S(1)}) all-reduce(f32[4]{0:T(128)S(1)} %get-tuple-element.315, f32[4]{0:T(128)S(1)} %get-tuple-element.314), channel_id=1, replica_groups=mesh['blk'=64,'probe'=4] {'blk'}, use_global_device_ids=true, to_apply=%region_1.0 | all-reduce | flops 8 | bytes 64 | tf_op jit(solution)/shard_map/psum | solution.py:42
  655.5 152.3 %psum.37 = f32[4]{0:T(128)S(1)} all-reduce(f32[4]{0:T(128)S(1)} %multiply_reduce_fusion.5), channel_id=1, replica_groups=mesh['blk'=64,'probe'=4] {'blk'}, use_global_device_ids=true, to_apply=%region_9.0 | all-reduce | flops 4 | bytes 32 | tf_op jit(solution)/shard_map/psum | solution.py:50
  808.0 153.5 %all_gather.16 = bf16[4,40960]{1,0:T(4,128)(2,1)S(1)} all-gather(bf16[4,640]{1,0:T(4,128)(2,1)S(1)} %get-tuple-element.344), channel_id=1, replica_groups=mesh['blk'=64,'probe'=4] {'blk'}, dimensions={1}, use_global_device_ids=true | all-gather | bytes 332800 | tf_op jit(solution)/shard_map/all_gather | solution.py:73
  961.5 182.2 %while.33 = (s32[]{:T(128)}, f32[4,640]{1,0:T(4,128)S(1)}, bf16[4,40960]{1,0:T(4,128)(2,1)S(1)}, f32[8,40960]{1,0:T(8,128)}, f32[640]{0:T(1024)S(1)}, /*index=5*...) while((s32[]{:T(128)}, f32[4,640]{1,0:T(4,128)S(1)}, ...), condition=%wide.region_12.13_spmd.clone, body=%wide.region_10.12_spmd.clone.sunk | while | flops 71454720 | bytes 2747057 | solution.py:38
  980.5 3.5 exponential_convert_fusion.5
  985.1 3.5 exponential_convert_fusion.5
  998.7 3.5 exponential_convert_fusion.5
  1007.8 3.5 exponential_convert_fusion.5
  1016.9 3.5 exponential_convert_fusion.5
  1026.1 3.5 exponential_convert_fusion.5
  1035.2 3.5 exponential_convert_fusion.5
  1044.3 3.5 exponential_convert_fusion.5
  1053.4 3.5 exponential_convert_fusion.5
  1062.5 3.5 exponential_convert_fusion.5
  1071.6 3.5 exponential_convert_fusion.5
  1080.7 3.5 exponential_convert_fusion.5
  1089.8 3.5 exponential_convert_fusion.5
  1098.9 3.5 exponential_convert_fusion.5
  1108.1 3.5 exponential_convert_fusion.5
  1117.2 3.5 exponential_convert_fusion.5
  1126.3 3.5 exponential_convert_fusion.5
  1135.4 3.5 exponential_convert_fusion.5
  1143.8 152.4 %psum.38 = f32[4]{0:T(128)S(1)} all-reduce(f32[4]{0:T(128)S(1)} %multiply_reduce_fusion.4), channel_id=1, replica_groups=mesh['blk'=64,'probe'=4] {'blk'}, use_global_device_ids=true, to_apply=%region_14.0 | all-reduce | flops 4 | bytes 32 | tf_op jit(solution)/shard_map/psum | solution.py:46
  1297.1 154.3 %psum.39 = f32[4]{0:T(128)S(1)} all-reduce(f32[4]{0:T(128)S(1)} %get-tuple-element.342), channel_id=1, replica_groups=mesh['blk'=64,'probe'=4] {'blk'}, use_global_device_ids=true, to_apply=%region_16.0 | all-reduce | flops 4 | bytes 32 | tf_op jit(solution)/shard_map/psum | solution.py:50
  (227 shorter events, 236.7 us)
Async XLA Ops:
  7.2 308.6 %all-gather.3.cloned.1.call-start = ((), (), s32[]{:S(2)}) async-start(), calls=%async_computation | async-start | bytes 1331200 | tf_op jit(solution)/shard_map/all_gather | solution.py:72
  1297.0 155.6 %copy-start = (f32[4,640]{1,0:T(4,128)}, f32[4,640]{1,0:T(4,128)S(1)}, u32[]{:S(2)}) copy-start(f32[4,640]{1,0:T(4,128)S(1)} %get-tuple-element.343) | copy-start | bytes 30724
Sparse Core Ops, SparseCore 0:
  15.0 300.7 all-gather.2
where the time goes:
time: 1470 us; the launch traced here: 1460 us
  blocking collectives  937 us (64%)
  matrix products  301 us (20%)
  waiting for transfers between devices  138 us (9%)
  other arithmetic  66.4 us (5%)
    all_gather x2, blocking collectives, on_device(): lax.all_gather(direction.astype(jnp.bfloat16).astype(jnp.float32), 'blk',...  314 us
    psum x2, blocking collectives, norm_total(): return lax.psum(values, 'blk')  307 us
    dot_general x80, matrix products, kernel_product(): lax.dot_general(other_points, own_points, (((0,), (0,)), ((), ())), preci...  278 us
    psum x1, blocking collectives, start_total(): return lax.psum(values, 'blk')  157 us
    psum x1, blocking collectives, curv_total(): return lax.psum(values, 'blk')  152 us
    all_gather x1, waiting for transfers between devices, on_device(): lax.all_gather(own_points, 'blk', axis=1, tiled=True)  138 us
    reduce_sum x80, other arithmetic, kernel_product(): norm_other = jnp.sum(other_points * other_points, 0)  62.2 us
  transfers between devices with their start and end apart: 1, of which 1 were waited for; matrix products, arithmetic and copies ran while one was open for 0% of the time, Pallas kernels for 0%

commit v1 on v0

v1 whole, which is shorter than its diff:
```python
import jax
import jax.numpy as jnp
from jax import lax
from jax.experimental import pallas as pl
from jax.experimental.pallas import tpu as pltpu
from jax.sharding import PartitionSpec as P

COLS = 16
FEAT = 8
LANES = 128
DEPTH = 64
LOG2E = 1.4426950408889634


def split3(value):
    high = value.astype(jnp.bfloat16).astype(jnp.float32)
    rest = value - high
    mid = rest.astype(jnp.bfloat16).astype(jnp.float32)
    return high, mid, rest - mid


def norm_rows(norm, ones_first):
    high, mid, low = split3(norm)
    row = lax.broadcasted_iota(jnp.int32, (8, norm.shape[1]), 0)
    at = 3 if ones_first else 0
    value = jnp.where(row == at, high, jnp.where(row == at + 1, mid, jnp.where(row == at + 2, low, 0.0)))
    other = (row < 3) if ones_first else ((row >= 3) & (row < 6))
    return jnp.where(other, 1.0, value)


def left_rows(points):
    high, mid, low = split3(points)
    norm = (-0.5 * LOG2E) * jnp.sum(points * points, 0, keepdims=True)
    extra = norm_rows(norm, True)
    return jnp.concatenate([high, high, high, mid, mid, low, extra, jnp.zeros_like(extra)], 0)


def right_rows(points):
    high, mid, low = split3(points * LOG2E)
    norm = (-0.5 * LOG2E) * jnp.sum(points * points, 0, keepdims=True)
    extra = norm_rows(norm, False)
    return jnp.concatenate([high, mid, low, high, mid, high, extra, jnp.zeros_like(extra)], 0)


def join_rest(parts, group):
    lane = lax.broadcasted_iota(jnp.int32, (8, LANES), 1)
    out = None
    for at, part in enumerate(parts):
        turn = (32 * (at - group)) % LANES
        moved = pltpu.roll(part, turn, 1) if turn else part
        out = moved if out is None else jnp.where(lane >= 32 * at, moved, out)
    return out


def tile_kernel(own_ref, got_ref, tile_ref, image_ref, right_ref):
    rows = right_rows(own_ref[...])
    right_ref[...] = jnp.transpose(jnp.concatenate([rows, jnp.zeros_like(rows)], 0)).astype(jnp.bfloat16)
    image_ref[...] = jnp.zeros_like(image_ref)
    blocks = got_ref.shape[0]

    def step(points_list, rhs_list, offset):
        left = jnp.concatenate([left_rows(q) for q in points_list], 1).astype(jnp.bfloat16)
        rhs = jnp.concatenate(rhs_list, 1).astype(jnp.bfloat16)
        power = jnp.dot(right_ref[:, :DEPTH], left, preferred_element_type=jnp.float32)
        tile = jnp.exp2(power).astype(jnp.bfloat16)
        tile_ref[:, pl.ds(pl.multiple_of(offset, 2 * LANES), 2 * LANES)] = tile
        image_ref[...] += lax.dot_general(rhs, tile, (((1,), (1,)), ((), ())), preferred_element_type=jnp.float32)

    def main(pair, carry):
        first = 2 * pair
        step(
            [got_ref[first + k, 0:8, :] for k in range(2)],
            [got_ref[first + k, 8:24, :] for k in range(2)],
            pair * (2 * LANES),
        )
        return carry

    lax.fori_loop(0, blocks // 2, main, 0)

    def rest(pair, carry):
        points_list, rhs_list = [], []
        for k in range(2):
            parts = [got_ref[8 * pair + 4 * k + q, 24:32, :] for q in range(4)]
            points_list.append(join_rest(parts, 0))
            rhs_list.append(jnp.concatenate([join_rest(parts, 1), join_rest(parts, 2)], 0))
        step(points_list, rhs_list, (blocks + 2 * pair) * LANES)
        return carry

    lax.fori_loop(0, blocks // 8, rest, 0)


def totals(stats):
    curv = pltpu.roll(stats, LANES - 2, 2)
    quad = pltpu.roll(stats, LANES - 4, 2)
    left = pltpu.roll(stats, LANES - 6, 2)
    norm = jnp.sum(stats, 0)
    step = norm / jnp.sum(curv, 0)
    best = jnp.where(quad > 0.0, curv / jnp.where(quad > 0.0, quad, 1.0), 0.0)
    gap = step[None] - best
    ratio = jnp.sum(left + gap * gap * quad, 0) / norm
    column = lambda v: jnp.concatenate([v[:, 64:65], v[:, 65:66]], 0)
    return column(step), column(ratio)


def second_kernel(got_ref, image_ref, tile_ref, out_ref, coeff_ref, dir_ref):
    blocks = got_ref.shape[0]
    step, ratio = totals(image_ref[:, 16:24, :])
    lane = lax.broadcasted_iota(jnp.int32, (COLS, LANES), 1)
    coeff_ref[...] = jnp.where(lane == 0, step, jnp.where(lane == 1, ratio, 0.0))

    def put(rhs, image, block):
        new = (rhs - step * image) + ratio * rhs
        dir_ref[:, pl.ds(pl.multiple_of(block * LANES, LANES), LANES)] = new.astype(jnp.bfloat16)

    def main(block, carry):
        put(got_ref[block, 8:24, :], image_ref[block, 0:16, :], block)
        return carry

    lax.fori_loop(0, blocks, main, 0)

    def rest(group, carry):
        parts = [got_ref[4 * group + q, 24:32, :] for q in range(4)]
        images = [image_ref[4 * group + q, 16:24, :] for q in range(4)]
        put(
            jnp.concatenate([join_rest(parts, 1), join_rest(parts, 2)], 0),
            jnp.concatenate([join_rest(images, 0), join_rest(images, 1)], 0),
            blocks + group,
        )
        return carry

    lax.fori_loop(0, blocks // 4, rest, 0)

    out_ref[...] = jnp.zeros_like(out_ref)
    width = 1024

    def chunk(at, carry):
        cols = pl.ds(pl.multiple_of(at * width, width), width)
        out_ref[...] += lax.dot_general(
            dir_ref[:, cols], tile_ref[:, cols], (((1,), (1,)), ((), ())), preferred_element_type=jnp.float32
        )
        return carry

    lax.fori_loop(0, tile_ref.shape[1] // width, chunk, 0)


VMEM = pl.BlockSpec(memory_space=pltpu.VMEM)


def first_product(own, got):
    rows, points = own.shape[1], got.shape[0] * 160
    return pl.pallas_call(
        tile_kernel,
        out_shape=(
            jax.ShapeDtypeStruct((rows, points), jnp.bfloat16),
            jax.ShapeDtypeStruct((COLS, rows), jnp.float32),
        ),
        in_specs=[VMEM, VMEM],
        out_specs=(VMEM, VMEM),
        scratch_shapes=[pltpu.VMEM((rows, LANES), jnp.bfloat16)],
        compiler_params=pltpu.CompilerParams(vmem_limit_bytes=40 * 2**20),
        name="tile_product",
    )(own, got)


def second_product(got, image, tile):
    rows, points = tile.shape
    return pl.pallas_call(
        second_kernel,
        out_shape=(
            jax.ShapeDtypeStruct((COLS, rows), jnp.float32),
            jax.ShapeDtypeStruct((COLS, LANES), jnp.float32),
        ),
        in_specs=[VMEM, VMEM, VMEM],
        out_specs=(VMEM, VMEM),
        scratch_shapes=[pltpu.VMEM((COLS, points), jnp.bfloat16)],
        compiler_params=pltpu.CompilerParams(vmem_limit_bytes=40 * 2**20),
        name="second_product",
    )(got, image, tile)


def swap(value, bit):
    return lax.ppermute(value, "probe", [(i, i ^ bit) for i in range(4)])


def probe_total(value):
    value = value + swap(value, 1)
    return value + swap(value, 2)


def to_all_blocks(piece):
    blocks = lax.axis_size("blk")
    return lax.all_to_all(jnp.broadcast_to(piece[None], (blocks,) + piece.shape), "blk", 0, 0)


def side_by_side(groups):
    width = sum(g.shape[1] for g in groups)
    return jnp.concatenate([*groups, jnp.zeros((8, LANES - width), jnp.float32)], 1)


def block_sums(residual, image):
    norm = jnp.sum(residual * residual, 1, keepdims=True)
    curv = jnp.sum(residual * image, 1, keepdims=True)
    quad = jnp.sum(image * image, 1, keepdims=True)
    return norm, curv, quad


def on_device(points, targets, signs):
    place = lax.axis_index("probe")
    quarter = points.shape[1]
    rhs = jnp.concatenate([targets[None, :], 2.0 * signs.astype(jnp.float32) - 1.0], 0)
    lane = lax.broadcasted_iota(jnp.int32, (FEAT, 4 * quarter), 1)
    mine = jnp.where(lane // quarter == place, jnp.concatenate([points] * 4, 1), 0.0)
    own = probe_total(mine)

    def own_quarter(value):
        return lax.dynamic_slice_in_dim(value, place * quarter, quarter, 1)

    rhs_q = own_quarter(rhs)
    piece = jnp.concatenate(
        [
            points[:, :LANES],
            rhs_q[:, :LANES],
            side_by_side([points[:, LANES:], rhs_q[:8, LANES:], rhs_q[8:, LANES:]]),
        ],
        0,
    )
    got = to_all_blocks(piece)
    tile, partial = first_product(own, got)

    image = probe_total(partial) + 0.5 * rhs
    norm, curv, quad = block_sums(rhs, image)
    best = jnp.where(quad > 0.0, curv / jnp.where(quad > 0.0, quad, 1.0), 0.0)
    left = jnp.sum(jnp.square(rhs - best * image), 1, keepdims=True)
    image_q = own_quarter(image)
    stats = [part for value in (norm, curv, quad, left) for part in (value[:8], value[8:])]
    piece = jnp.concatenate(
        [image_q[:, :LANES], side_by_side([image_q[:8, LANES:], image_q[8:, LANES:], *stats])], 0
    )
    images = to_all_blocks(piece)
    partial, coeff = second_product(got, images, tile)

    step, ratio = coeff[:, 0:1], coeff[:, 1:2]
    residual = rhs - step * image
    direction = residual + ratio * rhs
    image = probe_total(partial) + 0.5 * direction
    norm = jnp.sum(residual * residual, 1, keepdims=True)
    curv = jnp.sum(direction * image, 1, keepdims=True)
    cross = jnp.sum(residual * image, 1, keepdims=True)
    quad = jnp.sum(image * image, 1, keepdims=True)
    best = jnp.where(quad > 0.0, cross / jnp.where(quad > 0.0, quad, 1.0), 0.0)
    left = jnp.sum(jnp.square(residual - best * image), 1, keepdims=True)
    stats = jnp.concatenate([norm, curv, quad, best, left], 1)
    stats = side_by_side([stats[:8], stats[8:]])
    sums = to_all_blocks(stats)
    sums = jnp.concatenate([sums[:, :, 0:5], sums[:, :, 5:10]], 1)
    norm_now = jnp.sum(sums[:, :, 0], 0)[:, None]
    step_two = norm_now / jnp.sum(sums[:, :, 1], 0)[:, None]
    gap = step_two[None, :, 0] - sums[:, :, 3]
    norm_next = jnp.sum(sums[:, :, 4] + gap * gap * sums[:, :, 2], 0)[:, None]
    ratio_two = norm_next / norm_now

    def own_cols(value):
        return lax.dynamic_slice_in_dim(value, place * 4, 4, 0)

    direction, image, residual, rhs = map(own_cols, (direction, image, residual, rhs))
    step, ratio, step_two, ratio_two = map(own_cols, (step, ratio, step_two, ratio_two))
    answer = step * rhs + step_two * direction
    residual = residual - step_two * image
    direction = residual + ratio_two * direction
    coeffs = jnp.stack([jnp.stack([step[:, 0], step_two[:, 0]]), jnp.stack([ratio[:, 0], ratio_two[:, 0]])])
    return (answer, residual, direction, coeffs)


def solution(mesh):
    placed = (P(None, ("blk", "probe")), P("blk"), P(None, "blk"))
    return jax.shard_map(
        on_device,
        mesh=mesh,
        in_specs=placed,
        out_specs=(P("probe", "blk"), P("probe", "blk"), P("probe", "blk"), P(None, None, "probe")),
        check_vma=False,
    )
```

time: 1470 us -> 146 us (0.10)
  blocking collectives: 937 us -> 28.2 us
  matrix products: 301 us -> 0 us
  waiting for transfers between devices: 138 us -> 50.5 us
  other arithmetic: 66.4 us -> 5.27 us
  Pallas kernels: 0 us -> 29.4 us
  starting transfers between devices: 0.04 us -> 20.4 us
    psum x4 -> x0, blocking collectives: 616 us -> none  [the longest x2 307 us: norm_total(): return lax.psum(values, 'blk')]
    all_gather x3 -> x0, blocking collectives: 321 us -> none  [the longest x2 314 us: on_device(): lax.all_gather(direction.astype(jnp.bfloat16).astype(jnp.float32), 'blk',...]
    dot_general x160 -> x0, matrix products: 301 us -> none  [the longest x80 278 us: kernel_product(): lax.dot_general(other_points, own_points, (((0,), (0,)), ((), ())), preci...]
    all_gather x1 -> x0, waiting for transfers between devices: 138 us -> none  [on_device(): lax.all_gather(own_points, 'blk', axis=1, tiled=True)]
    reduce_sum x85 -> x6, other arithmetic: 64.2 us -> 1.04 us  [the longest x1 0.22 us: on_device(): left = jnp.sum(jnp.square(residual - best * image), 1, keepdims=True)]
    all_to_all x0 -> x2, waiting for transfers between devices: none -> 32.5 us  [to_all_blocks(): lax.all_to_all(jnp.broadcast_to(piece[None], (blocks,) + piece.shape), 'b...]
    pallas_call x0 -> x2, Pallas kernels: none -> 29.4 us  [the longest x1 17.9 us: first_product(): pl.pallas_call(tile_kernel, out_shape=(jax.ShapeDtypeStruct((rows, points...]
    all_to_all x0 -> x1, blocking collectives: none -> 28.2 us  [to_all_blocks(): lax.all_to_all(jnp.broadcast_to(piece[None], (blocks,) + piece.shape), 'b...]
  transfers between devices with their start and end apart: 1 -> 8, of which waited for: 1 -> 8; matrix products, arithmetic and copies ran while one was open for 0% -> 2% of each run, Pallas kernels for 0% -> 0%
where the time goes in v1:
time: 146 us
  waiting for transfers between devices  50.5 us (35%)
  Pallas kernels  29.4 us (20%)
  blocking collectives  28.2 us (19%)
  starting transfers between devices  20.4 us (14%)
  local copies, waits for them, and re-layouts  11.3 us (8%)
  other arithmetic  5.27 us (4%)
    all_to_all x2, waiting for transfers between devices, to_all_blocks(): lax.all_to_all(jnp.broadcast_to(piece[None], (blocks,) + piece.shape), 'b...  32.5 us
    all_to_all x1, blocking collectives, to_all_blocks(): lax.all_to_all(jnp.broadcast_to(piece[None], (blocks,) + piece.shape), 'b...  28.2 us
    all_to_all x2, starting transfers between devices, to_all_blocks(): lax.all_to_all(jnp.broadcast_to(piece[None], (blocks,) + piece.shape), 'b...  18.3 us
    ppermute x6, waiting for transfers between devices, swap(): return lax.ppermute(value, 'probe', [(i, i ^ bit) for i in range(4)])  17.9 us
    pallas_call x1, Pallas kernels, first_product(): pl.pallas_call(tile_kernel, out_shape=(jax.ShapeDtypeStruct((rows, points...  17.9 us
    pallas_call x1, Pallas kernels, second_product(): pl.pallas_call(second_kernel, out_shape=(jax.ShapeDtypeStruct((COLS, rows...  11.5 us
    unnamed x4, local copies, waits for them, and re-layouts  4.97 us
  transfers between devices with their start and end apart: 8, of which 8 were waited for; matrix products, arithmetic and copies ran while one was open for 2% of the time, Pallas kernels for 0%

profile of v1, /device:TPU:16, one launch (start us, length us, event | category | flops | bytes accessed | tf_op | source)
XLA Modules:
  0.0 145.8 jit_solution(2887544827326321337)
XLA Ops:
  0.6 0.8 multiply_add_fusion.3
  1.4 0.7 broadcast_in_dim.63
  2.2 0.7 slice.105
  2.9 0.7 slice.107
  3.7 1.1 broadcast_in_dim.65
  4.8 12.7 %all-to-all-start = ((f32[64,32,128]{2,1,0:T(8,128)}), f32[64,32,128]{2,1,0:T(8,128)S(1)}, u32[]{:S(2)}, u32[]{:S(2)}) async-start(f32[64,32,128]{2,1,0:T(8,128)} %broadcast_in_dim.65), calls=%async_computation | async-start | bytes 2097152 | tf_op jit(solution)/shard_map/all_to_all | solution.py:192
  17.5 0.9 maximum_select_fusion
  18.4 1.2 collective-permute-done
  19.6 0.9 fusion.26
  20.5 0.7 collective-permute-start.1
  21.2 4.9 %collective-permute-done.1 = f32[8,640]{1,0:T(8,128)S(1)} collective-permute-done((f32[8,640]{1,0:T(8,128)S(1)}, f32[8,640]{1,0:T(8,128)S(1)}, u32[]{:S(2)}, u32[]{:S(2)}) %collective-permute-start.1) | collective-permute-done | bytes 20512 | tf_op jit(solution)/shard_map/ppermute | solution.py:182
  26.1 20.3 %all-to-all-done.got_ref = f32[64,32,128]{2,1,0:T(8,128)S(1)} async-done(((f32[64,32,128]{2,1,0:T(8,128)}), f32[64,32,128]{2,1,0:T(8,128)S(1)}, u32[]{:S(2)}, u32[]{:S(2)}) %all-to-all-start) | async-done | bytes 1048608 | tf_op jit(solution)/shard_map/all_to_all | solution.py:192
  46.4 17.9 %tile_product.1 = (bf16[640,10240]{1,0:T(8,128)(2,1)S(1)}, f32[16,640]{1,0:T(8,128)S(1)}) custom-call(f32[8,640]{1,0:T(8,128)S(1)} %add.55.own_ref, f32[64,32,128]{2,1,0:T(8,128)S(1)} %all-to-all-done.got_ref), custom_call_target="tpu_custom_call" | custom-call | tf_op jit(solution)/shard_map/tile_product/pallas_call | solution.py:151
  64.3 4.7 %copy-done = bf16[640,10240]{1,0:T(8,128)(2,1)} copy-done((bf16[640,10240]{1,0:T(8,128)(2,1)}, bf16[640,10240]{1,0:T(8,128)(2,1)S(1)}, u32[]{:S(2)}) %copy-start) | copy-done | bytes 13107224
  69.0 1.2 collective-permute-done.2
  70.2 0.6 collective-permute-start.3
  70.9 4.9 %collective-permute-done.3 = f32[16,640]{1,0:T(8,128)S(1)} collective-permute-done((f32[16,640]{1,0:T(8,128)S(1)}, f32[16,640]{1,0:T(8,128)S(1)}, u32[]{:S(2)}, u32[]{:S(2)}) %collective-permute-start.3) | collective-permute-done | bytes 40992 | tf_op jit(solution)/shard_map/ppermute | solution.py:182
  75.7 0.1 multiply_reduce_fusion.6
  76.1 0.2 multiply_reduce_fusion.5
  76.4 0.1 copy.27
  76.4 0.1 copy.28
  76.6 0.1 copy.33
  76.7 0.1 copy.34
  76.8 0.1 copy.29
  76.8 0.1 copy.30
  77.0 0.1 copy.32
  77.2 0.1 concatenate.31
  77.3 28.2 %all_to_all.15.image_ref = f32[64,24,128]{2,1,0:T(8,128)S(1)} all-to-all(f32[64,24,128]{2,1,0:T(8,128)S(1)} %broadcast_in_dim.69), channel_id=1, replica_groups=mesh['blk'=64,'probe'=4] {'blk'}, dimensions={0} | all-to-all | bytes 1572864 | tf_op jit(solution)/shard_map/all_to_all | solution.py:192
  105.5 11.5 %second_product.1 = (f32[16,640]{1,0:T(8,128)S(1)}, f32[16,128]{1,0:T(8,128)S(1)}) custom-call(f32[64,32,128]{2,1,0:T(8,128)S(1)} %all-to-all-done.got_ref, f32[64,24,128]{2,1,0:T(8,128)S(1)} %all_to_all.15.image_ref, bf16[640,10240]{1,0:T(8,128)(2,1)} %copy-done), custom_call_target="tpu_custom_call" | custom-call | tf_op jit(solution)/shard_map/second_product/pallas_call | solution.py:167
  117.2 1.1 collective-permute-done.4
  118.3 0.6 collective-permute-start.5
  118.9 0.2 slice_reduce_fusion
  119.1 4.7 %collective-permute-done.5 = f32[16,640]{1,0:T(8,128)S(1)} collective-permute-done((f32[16,640]{1,0:T(8,128)S(1)}, f32[16,640]{1,0:T(8,128)S(1)}, u32[]{:S(2)}, u32[]{:S(2)}) %collective-permute-start.5) | collective-permute-done | bytes 40992 | tf_op jit(solution)/shard_map/ppermute | solution.py:182
  123.8 0.2 multiply_reduce_fusion.1
  124.0 0.2 multiply_reduce_fusion
  124.4 0.1 copy.36
  124.6 0.7 broadcast_in_dim.76
  125.3 5.7 %all-to-all-start.2 = ((f32[64,8,128]{2,1,0:T(8,128)}), f32[64,8,128]{2,1,0:T(8,128)S(1)}, u32[]{:S(2)}, u32[]{:S(2)}) async-start(f32[64,8,128]{2,1,0:T(8,128)} %broadcast_in_dim.76), calls=%async_computation.2 | async-start | bytes 524288 | tf_op jit(solution)/shard_map/all_to_all | solution.py:192
  131.0 0.1 fusion.21
  131.1 0.1 fusion.22
  131.2 12.2 %all-to-all-done.2 = f32[64,8,128]{2,1,0:T(8,128)S(1)} async-done(((f32[64,8,128]{2,1,0:T(8,128)}), f32[64,8,128]{2,1,0:T(8,128)S(1)}, u32[]{:S(2)}, u32[]{:S(2)}) %all-to-all-start.2) | async-done | bytes 262176 | tf_op jit(solution)/shard_map/all_to_all | solution.py:192
  143.4 0.1 fusion.27
  143.6 0.1 copy.39
  143.7 0.2 copy.40
  143.9 0.1 fusion.13
  144.1 0.2 fusion.17
  144.6 0.6 pad_maximum_fusion.3
  145.1 0.7 multiply_add_fusion.4
  (41 shorter events, 1.6 us)
Async XLA Ops:
  4.8 41.6 %all-to-all-start = ((f32[64,32,128]{2,1,0:T(8,128)}), f32[64,32,128]{2,1,0:T(8,128)S(1)}, u32[]{:S(2)}, u32[]{:S(2)}) async-start(f32[64,32,128]{2,1,0:T(8,128)} %broadcast_in_dim.65), calls=%async_computation | async-start | bytes 2097152 | tf_op jit(solution)/shard_map/all_to_all | solution.py:192
  18.4 1.2 collective-permute-start
  20.5 5.6 %collective-permute-start.1 = (f32[8,640]{1,0:T(8,128)S(1)}, f32[8,640]{1,0:T(8,128)S(1)}, u32[]{:S(2)}, u32[]{:S(2)}) collective-permute-start(f32[8,640]{1,0:T(8,128)S(1)} %fusion.26), channel_id=1, source_target_pairs={{0,2},{1,3},{2,0},{3,1},{4,6},{5,7},{6,4},{7,5},{8,10},{9,11},{10,... | collective-permute-start | bytes 61448 | tf_op jit(solution)/shard_map/ppermute | solution.py:182
  64.3 4.7 %copy-start = (bf16[640,10240]{1,0:T(8,128)(2,1)}, bf16[640,10240]{1,0:T(8,128)(2,1)S(1)}, u32[]{:S(2)}) copy-start(bf16[640,10240]{1,0:T(8,128)(2,1)S(1)} %get-tuple-element.9.tile_ref) | copy-start | bytes 39321604
  69.0 1.2 collective-permute-start.2
  70.2 5.5 %collective-permute-start.3 = (f32[16,640]{1,0:T(8,128)S(1)}, f32[16,640]{1,0:T(8,128)S(1)}, u32[]{:S(2)}, u32[]{:S(2)}) collective-permute-start(f32[16,640]{1,0:T(8,128)S(1)} %add.56), channel_id=1, source_target_pairs={{0,2},{1,3},{2,0},{3,1},{4,6},{5,7},{6,4},{7,5},{8,10},{9,11},{10,... | collective-permute-start | bytes 122888 | tf_op jit(solution)/shard_map/ppermute | solution.py:182
  117.0 1.3 collective-permute-start.4
  118.3 5.5 %collective-permute-start.5 = (f32[16,640]{1,0:T(8,128)S(1)}, f32[16,640]{1,0:T(8,128)S(1)}, u32[]{:S(2)}, u32[]{:S(2)}) collective-permute-start(f32[16,640]{1,0:T(8,128)S(1)} %add.61), channel_id=1, source_target_pairs={{0,2},{1,3},{2,0},{3,1},{4,6},{5,7},{6,4},{7,5},{8,10},{9,11},{10,... | collective-permute-start | bytes 122888 | tf_op jit(solution)/shard_map/ppermute | solution.py:182
  125.3 18.1 %all-to-all-start.2 = ((f32[64,8,128]{2,1,0:T(8,128)}), f32[64,8,128]{2,1,0:T(8,128)S(1)}, u32[]{:S(2)}, u32[]{:S(2)}) async-start(f32[64,8,128]{2,1,0:T(8,128)} %broadcast_in_dim.76), calls=%async_computation.2 | async-start | bytes 524288 | tf_op jit(solution)/shard_map/all_to_all | solution.py:192

commit v2 on v0

v2 whole, which is shorter than its diff:
```python
import jax
import jax.numpy as jnp
from jax import lax
from jax.experimental import pallas as pl
from jax.experimental.pallas import tpu as pltpu
from jax.sharding import PartitionSpec as P

COLS = 16
FEAT = 8
LANES = 128
REST = 32
DEPTH = 48
WIDTH = 1024
LOG2E = 1.4426950408889634
LIMIT = 24 * 2**20


def rounded(value):
    return value.astype(jnp.bfloat16).astype(jnp.float32)


def split3(value):
    high = rounded(value)
    mid = rounded(value - high)
    return high, mid, value - high - mid


def norm_rows(points, ones_first):
    high, mid, low = split3((-0.5 * LOG2E) * jnp.sum(points * points, 0, keepdims=True))
    row = lax.broadcasted_iota(jnp.int32, points.shape, 0)
    at = 3 if ones_first else 0
    value = jnp.where(row == at, high, jnp.where(row == at + 1, mid, jnp.where(row == at + 2, low, 0.0)))
    other = (row < 3) if ones_first else ((row >= 3) & (row < 6))
    return jnp.where(other, 1.0, value)


def left_rows(high, low):
    return jnp.concatenate([high, high, high, low, low, norm_rows(high + low, True)], 0)


def right_rows(points):
    high = rounded(points)
    points = high + rounded(points - high)
    top, mid, end = split3(points * LOG2E)
    return jnp.concatenate([top, mid, end, top, mid, norm_rows(points, False)], 0)


def lane_of(shape):
    return lax.broadcasted_iota(jnp.int32, shape, len(shape) - 1)


def turn(value, by):
    by = by % value.shape[-1]
    return pltpu.roll(value, by, value.ndim - 1) if by else value


def pack_rest(groups):
    lane = lane_of((8, LANES))
    out = jnp.zeros((8, LANES), jnp.float32)
    for at, group in enumerate(groups):
        out = jnp.where((lane >= REST * at) & (lane < REST * (at + 1)), turn(group, REST * at), out)
    return out


def join_rest(parts, group):
    lane = lane_of((8, LANES))
    out = None
    for at, part in enumerate(parts):
        moved = turn(part, REST * (at - group))
        out = moved if out is None else jnp.where(lane >= REST * at, moved, out)
    return out


def repeat_piece(ref, piece):
    piece = piece.astype(ref.dtype)

    def put(block, carry):
        ref[block] = piece
        return carry

    lax.fori_loop(0, ref.shape[0], put, 0, unroll=8)


def pack_kernel(place_ref, points_ref, targets_ref, signs_ref, piece_ref, rhs_ref, mine_ref):
    place = place_ref[0]
    quarter = points_ref.shape[1]
    rhs_ref[0:1, :] = targets_ref[...]
    rhs_ref[1:COLS, :] = 2.0 * signs_ref[...].astype(jnp.float32) - 1.0
    mine_ref[...] = jnp.zeros_like(mine_ref)
    mine_ref[:, 0:quarter] = points_ref[...]
    points = mine_ref[...]
    mine_ref[...] = pltpu.roll(points, place * quarter, 1)
    width = rhs_ref.shape[1]
    rhs = pltpu.roll(rhs_ref[...], lax.rem(width - place * quarter, width), 1)
    high = rounded(points)
    low = rounded(points - high)
    ends = slice(LANES, 2 * LANES)
    rest = pack_rest([rhs[:8, ends], rhs[8:, ends], high[:, ends], low[:, ends]])
    repeat_piece(
        piece_ref, jnp.concatenate([high[:, :LANES], low[:, :LANES], rhs[:, :LANES], rest], 0)
    )


def tile_kernel(own_ref, got_ref, tile_ref, image_ref, right_ref, left_ref, rhs_ref):
    rows = right_rows(own_ref[...])
    pad = jnp.zeros((LANES - DEPTH, rows.shape[1]), jnp.float32)
    right_ref[...] = jnp.transpose(jnp.concatenate([rows, pad], 0)).astype(jnp.bfloat16)
    blocks = got_ref.shape[0]

    def put(left, rhs, block):
        cols = pl.ds(pl.multiple_of(block * LANES, LANES), LANES)
        left_ref[:, cols] = left.astype(jnp.bfloat16)
        rhs_ref[:, cols] = rhs.astype(jnp.bfloat16)

    def main(block, carry):
        piece = got_ref[block].astype(jnp.float32)
        put(left_rows(piece[0:8], piece[8:16]), piece[16:32], block)
        return carry

    lax.fori_loop(0, blocks, main, 0, unroll=8)

    def rest(group, carry):
        parts = [got_ref[4 * group + q].astype(jnp.float32)[32:40] for q in range(4)]
        joined = [join_rest(parts, g) for g in range(4)]
        put(left_rows(joined[2], joined[3]), jnp.concatenate(joined[:2], 0), blocks + group)
        return carry

    lax.fori_loop(0, blocks // 4, rest, 0, unroll=4)

    def step(at, total):
        cols = pl.ds(pl.multiple_of(at * WIDTH, WIDTH), WIDTH)
        power = jnp.dot(right_ref[:, :DEPTH], left_ref[:, cols], preferred_element_type=jnp.float32)
        tile = jnp.exp2(power).astype(jnp.bfloat16)
        tile_ref[:, cols] = tile
        return total + lax.dot_general(
            rhs_ref[:, cols], tile, (((1,), (1,)), ((), ())), preferred_element_type=jnp.float32
        )

    image_ref[...] = lax.fori_loop(0, tile_ref.shape[1] // WIDTH, step, jnp.zeros(image_ref.shape, jnp.float32), unroll=2)


def safe_ratio(top, bottom):
    good = bottom > 0.0
    return jnp.where(good, top / jnp.where(good, bottom, 1.0), 0.0)


def row_sum(value):
    return jnp.sum(value, 1, keepdims=True)


def send_kernel(place_ref, rhs_ref, near_ref, far_ref, piece_ref, image_ref):
    rhs = rhs_ref[...]
    image = near_ref[...] + far_ref[...] + 0.5 * rhs
    image_ref[...] = image
    norm, curv, quad = row_sum(rhs * rhs), row_sum(rhs * image), row_sum(image * image)
    left = row_sum(jnp.square(rhs - safe_ratio(curv, quad) * image))
    share = safe_ratio(curv, norm)
    width = rhs.shape[1]
    back = lax.rem(width - place_ref[0] * (width // 4), width)
    rest = pltpu.roll(image - share * rhs, back, 1)
    packed = pack_rest([rest[:8, LANES : 2 * LANES], rest[8:, LANES : 2 * LANES]])
    lane = lane_of((8, LANES))
    at = 2 * REST
    for value in (norm, curv, quad, left, share):
        for part in split3(value):
            for half in (part[:8], part[8:]):
                packed = jnp.where(lane == at, half, packed)
                at += 1
    repeat_piece(piece_ref, jnp.concatenate([rest[:, :LANES], packed], 0))


def second_kernel(got_ref, images_ref, tile_ref, out_ref, coeff_ref, dir_ref):
    blocks = got_ref.shape[0]

    def add(block, sums):
        norm, curv = sums
        value = images_ref[block].astype(jnp.float32)[16:24]
        value = value + turn(value, -2) + turn(value, -4)
        return norm + value, curv + turn(value, -6)

    zero = jnp.zeros((8, LANES), jnp.float32)
    norm, curv = lax.fori_loop(0, blocks, add, (zero, zero), unroll=8)
    step = norm / curv

    def grow(block, total):
        value = images_ref[block].astype(jnp.float32)[16:24]
        value = value + turn(value, -2) + turn(value, -4)
        quad = turn(value, -12)
        gap = step - safe_ratio(turn(value, -6), quad)
        return total + turn(value, -18) + gap * gap * quad

    ratio = lax.fori_loop(0, blocks, grow, zero, unroll=8) / norm
    at = 2 * REST

    def column(value):
        return jnp.concatenate([value[:, at : at + 1], value[:, at + 1 : at + 2]], 0)

    step_col, ratio_col = column(step), column(ratio)
    lane = lane_of((COLS, LANES))
    coeff_ref[...] = jnp.where(lane == 0, step_col, jnp.where(lane == 1, ratio_col, 0.0))
    lane = lane_of((8, LANES))

    def factor(block):
        value = images_ref[block].astype(jnp.float32)[16:24]
        value = turn(value + turn(value, -2) + turn(value, -4), -24)
        return (1.0 + ratio_col) - step_col * column(value)

    def put(value, block):
        dir_ref[:, pl.ds(pl.multiple_of(block * LANES, LANES), LANES)] = value.astype(jnp.bfloat16)

    def group_of_four(group, carry):
        ends = []
        for q in range(4):
            block = 4 * group + q
            piece = got_ref[block].astype(jnp.float32)
            image = images_ref[block].astype(jnp.float32)
            scale = factor(block)
            put(scale * piece[16:32] - step_col * image[:16], block)
            low = lane < REST
            ends.append(
                jnp.where(low, scale[:8], scale[8:]) * piece[32:40]
                - jnp.where(low, step_col[:8], step_col[8:]) * image[16:24]
            )
        put(jnp.concatenate([join_rest(ends, 0), join_rest(ends, 1)], 0), blocks + group)
        return carry

    lax.fori_loop(0, blocks // 4, group_of_four, 0, unroll=2)

    def chunk(at, total):
        cols = pl.ds(pl.multiple_of(at * WIDTH, WIDTH), WIDTH)
        return total + lax.dot_general(
            dir_ref[:, cols], tile_ref[:, cols], (((1,), (1,)), ((), ())), preferred_element_type=jnp.float32
        )

    out_ref[...] = lax.fori_loop(0, tile_ref.shape[1] // WIDTH, chunk, jnp.zeros(out_ref.shape, jnp.float32), unroll=5)


def sums_kernel(rhs_ref, image_ref, coeff_ref, near_ref, far_ref, piece_ref, res_ref, dir_ref, out_ref):
    rhs = rhs_ref[...]
    step, ratio = coeff_ref[:, 0:1], coeff_ref[:, 1:2]
    residual = rhs - step * image_ref[...]
    direction = residual + ratio * rhs
    image = near_ref[...] + far_ref[...] + 0.5 * direction
    res_ref[...], dir_ref[...], out_ref[...] = residual, direction, image
    quad = row_sum(image * image)
    best = safe_ratio(row_sum(residual * image), quad)
    left = row_sum(jnp.square(residual - best * image))
    values = (row_sum(residual * residual), row_sum(direction * image), quad, best, left)
    lane = lane_of((8, LANES))
    piece = jnp.zeros((8, LANES), jnp.float32)
    for at, value in enumerate(values):
        piece = jnp.where(lane == 2 * at, value[:8], jnp.where(lane == 2 * at + 1, value[8:], piece))
    repeat_piece(piece_ref, piece)


def last_kernel(place_ref, sums_ref, rhs_ref, res_ref, dir_ref, image_ref, coeff_ref,
                answer_ref, residual_ref, direction_ref, coeffs_ref):
    sums = sums_ref[...]
    total = jnp.sum(sums, 0)
    step = total / turn(total, -2)
    gap = step[None] - turn(sums, -6)
    ratio = jnp.sum(turn(sums, -8) + gap * gap * turn(sums, -4), 0) / total

    def column(value):
        return jnp.concatenate([value[:, 0:1], value[:, 1:2]], 0)

    step, ratio = column(step), column(ratio)
    direction = dir_ref[...]
    residual = res_ref[...] - step * image_ref[...]

    def own_cols(value):
        out = value[0:4]
        for at in range(1, 4):
            out = jnp.where(place_ref[0] == at, value[4 * at : 4 * at + 4], out)
        return out

    answer_ref[...] = own_cols(coeff_ref[:, 0:1] * rhs_ref[...] + step * direction)
    residual_ref[...] = own_cols(residual)
    direction_ref[...] = own_cols(residual + ratio * direction)
    lane = lane_of((COLS, LANES))
    coeffs_ref[...] = own_cols(jnp.where(lane == 2, step, jnp.where(lane == 3, ratio, coeff_ref[...])))


VMEM = pl.BlockSpec(memory_space=pltpu.VMEM)
SMEM = pl.BlockSpec(memory_space=pltpu.SMEM)


def call(kernel, outs, scratch, *args):
    return pl.pallas_call(
        kernel,
        out_shape=tuple(jax.ShapeDtypeStruct(shape, kind) for shape, kind in outs),
        in_specs=[SMEM if a.dtype == jnp.int32 and a.shape == (1,) else VMEM for a in args],
        out_specs=tuple(VMEM for _ in outs),
        scratch_shapes=[pltpu.VMEM(shape, kind) for shape, kind in scratch],
        compiler_params=pltpu.CompilerParams(vmem_limit_bytes=LIMIT),
        name=kernel.__name__,
    )(*args)


def swap(value, bit):
    return lax.ppermute(value, "probe", [(i, i ^ bit) for i in range(4)])


def to_all_blocks(pieces):
    return lax.all_to_all(pieces, "blk", 0, 0)


def on_device(points, targets, signs):
    blocks = lax.axis_size("blk")
    rows = targets.shape[0]
    others = blocks * points.shape[1]
    place = lax.axis_index("probe").astype(jnp.int32)[None]
    f32, bf16 = jnp.float32, jnp.bfloat16
    wide = ((COLS, rows), f32)

    pieces, rhs, mine = call(
        pack_kernel,
        [((blocks, 40, LANES), bf16), wide, ((FEAT, rows), f32)],
        [],
        place, points, targets[None, :], signs,
    )
    got = to_all_blocks(pieces)
    own = mine + swap(mine, 1)
    own = own + swap(own, 2)
    tile, part = call(
        tile_kernel,
        [((rows, others), bf16), wide],
        [((rows, LANES), bf16), ((DEPTH, others), bf16), ((COLS, others), bf16)],
        own, got,
    )
    near = part + swap(part, 1)
    pieces, image = call(
        send_kernel, [((blocks, 24, LANES), bf16), wide], [], place, rhs, near, swap(near, 2)
    )
    images = to_all_blocks(pieces)
    part, coeff = call(
        second_kernel, [wide, ((COLS, LANES), f32)], [((COLS, others), bf16)], got, images, tile
    )
    near = part + swap(part, 1)
    pieces, residual, direction, image = call(
        sums_kernel, [((blocks, 8, LANES), f32), wide, wide, wide], [], rhs, image, coeff, near, swap(near, 2)
    )
    sums = to_all_blocks(pieces)
    small = ((4, rows), f32)
    answer, residual, direction, coeff = call(
        last_kernel,
        [small, small, small, ((4, LANES), f32)],
        [],
        place, sums, rhs, residual, direction, image, coeff,
    )
    coeffs = jnp.stack([coeff[:, 0:3:2].T, coeff[:, 1:4:2].T])
    return (answer, residual, direction, coeffs)


def solution(mesh):
    placed = (P(None, ("blk", "probe")), P("blk"), P(None, "blk"))
    return jax.shard_map(
        on_device,
        mesh=mesh,
        in_specs=placed,
        out_specs=(P("probe", "blk"), P("probe", "blk"), P("probe", "blk"), P(None, None, "probe")),
        check_vma=False,
    )
```

time: 1470 us -> 109 us (0.07)
  blocking collectives: 937 us -> 37.6 us
  matrix products: 301 us -> 0 us
  waiting for transfers between devices: 138 us -> 32.2 us
  other arithmetic: 66.4 us -> 0.61 us
  Pallas kernels: 0 us -> 20.1 us
    psum x4 -> x0, blocking collectives: 616 us -> none  [the longest x2 307 us: norm_total(): return lax.psum(values, 'blk')]
    all_gather x3 -> x0, blocking collectives: 321 us -> none  [the longest x2 314 us: on_device(): lax.all_gather(direction.astype(jnp.bfloat16).astype(jnp.float32), 'blk',...]
    dot_general x160 -> x0, matrix products: 301 us -> none  [the longest x80 278 us: kernel_product(): lax.dot_general(other_points, own_points, (((0,), (0,)), ((), ())), preci...]
    all_gather x1 -> x0, waiting for transfers between devices: 138 us -> none  [on_device(): lax.all_gather(own_points, 'blk', axis=1, tiled=True)]
    reduce_sum x85 -> x0, other arithmetic: 64.2 us -> none  [the longest x80 62.2 us: kernel_product(): norm_other = jnp.sum(other_points * other_points, 0)]
    all_to_all x0 -> x2, blocking collectives: none -> 37.6 us  [to_all_blocks(): return lax.all_to_all(pieces, 'blk', 0, 0)]
    pallas_call x0 -> x6, Pallas kernels: none -> 20.1 us  [call(): pl.pallas_call(kernel, out_shape=tuple((jax.ShapeDtypeStruct(shape, kind)...]
    ppermute x0 -> x6, waiting for transfers between devices: none -> 18.3 us  [swap(): return lax.ppermute(value, 'probe', [(i, i ^ bit) for i in range(4)])]
  transfers between devices with their start and end apart: 1 -> 7, of which waited for: 1 -> 7; matrix products, arithmetic and copies ran while one was open for 0% -> 0% of each run, Pallas kernels for 0% -> 0%
where the time goes in v2:
time: 109 us; the launch traced here: 108 us
  blocking collectives  37.6 us (34%)
  waiting for transfers between devices  32.2 us (30%)
  Pallas kernels  20.1 us (18%)
  starting transfers between devices  14.6 us (13%)
  local copies, waits for them, and re-layouts  2.54 us (2%)
    all_to_all x2, blocking collectives, to_all_blocks(): return lax.all_to_all(pieces, 'blk', 0, 0)  37.6 us
    pallas_call x6, Pallas kernels, call(): pl.pallas_call(kernel, out_shape=tuple((jax.ShapeDtypeStruct(shape, kind)...  20.1 us
    ppermute x6, waiting for transfers between devices, swap(): return lax.ppermute(value, 'probe', [(i, i ^ bit) for i in range(4)])  18.3 us
    all_to_all x1, waiting for transfers between devices, to_all_blocks(): return lax.all_to_all(pieces, 'blk', 0, 0)  13.8 us
    all_to_all x1, starting transfers between devices, to_all_blocks(): return lax.all_to_all(pieces, 'blk', 0, 0)  12.7 us
  transfers between devices with their start and end apart: 7, of which 7 were waited for; matrix products, arithmetic and copies ran while one was open for 0% of the time, Pallas kernels for 0%

profile of v2, /device:TPU:16, one launch (start us, length us, event | category | flops | bytes accessed | tf_op | source)
XLA Modules:
  0.0 108.3 jit_solution(52306971367058502)
XLA Ops:
  0.6 0.7 broadcast_in_dim.7.targets_ref
  1.3 0.0 copy-start
  1.3 0.8 copy-done
  2.1 0.0 copy-start.1
  2.1 0.7 copy-done.1
  2.8 1.1 pack_kernel.1
  3.9 12.7 %all-to-all-start = ((bf16[64,40,128]{2,1,0:T(8,128)(2,1)}), bf16[64,40,128]{2,1,0:T(8,128)(2,1)S(1)}, u32[]{:S(2)}, u32[]{:S(2)}) async-start(bf16[64,40,128]{2,1,0:T(8,128)(2,1)} %get-tuple-element.23), calls=%async_computation | async-start | bytes 1310720 | tf_op jit(solution)/shard_map/all_to_all | solution.py:305
  16.5 0.1 collective-permute-start
  16.6 1.2 %collective-permute-done = f32[8,640]{1,0:T(8,128)S(1)} collective-permute-done((f32[8,640]{1,0:T(8,128)S(1)}, f32[8,640]{1,0:T(8,128)S(1)}, u32[]{:S(2)}, u32[]{:S(2)}) %collective-permute-start) | collective-permute-done | bytes 20512 | tf_op jit(solution)/shard_map/ppermute | solution.py:301
  17.8 0.6 collective-permute-start.1
  18.4 4.9 %collective-permute-done.1 = f32[8,640]{1,0:T(8,128)S(1)} collective-permute-done((f32[8,640]{1,0:T(8,128)S(1)}, f32[8,640]{1,0:T(8,128)S(1)}, u32[]{:S(2)}, u32[]{:S(2)}) %collective-permute-start.1) | collective-permute-done | bytes 20512 | tf_op jit(solution)/shard_map/ppermute | solution.py:301
  23.4 13.8 %all-to-all-done.got_ref = bf16[64,40,128]{2,1,0:T(8,128)(2,1)S(1)} async-done(((bf16[64,40,128]{2,1,0:T(8,128)(2,1)}), bf16[64,40,128]{2,1,0:T(8,128)(2,1)S(1)}, u32[]{:S(2)}, u32[]{:S(2)}) %all-to-all-start) | async-done | bytes 655392 | tf_op jit(solution)/shard_map/all_to_all | solution.py:305
  37.2 8.2 %tile_kernel.1 = (bf16[640,10240]{1,0:T(8,128)(2,1)S(1)}, f32[16,640]{1,0:T(8,128)S(1)}) custom-call(f32[8,640]{1,0:T(8,128)S(1)} %add.13.own_ref, bf16[64,40,128]{2,1,0:T(8,128)(2,1)S(1)} %all-to-all-done.got_ref), custom_call_target="tpu_custom_call" | custom-call | tf_op jit(solution)/shard_map/tile_kernel/pallas_call | solution.py:289
  45.4 0.0 collective-permute-start.2
  45.4 1.2 %collective-permute-done.2 = f32[16,640]{1,0:T(8,128)S(1)} collective-permute-done((f32[16,640]{1,0:T(8,128)S(1)}, f32[16,640]{1,0:T(8,128)S(1)}, u32[]{:S(2)}, u32[]{:S(2)}) %collective-permute-start.2) | collective-permute-done | bytes 40992 | tf_op jit(solution)/shard_map/ppermute | solution.py:301
  46.6 0.6 collective-permute-start.3
  47.3 4.9 %collective-permute-done.3.far_ref = f32[16,640]{1,0:T(8,128)S(1)} collective-permute-done((f32[16,640]{1,0:T(8,128)S(1)}, f32[16,640]{1,0:T(8,128)S(1)}, u32[]{:S(2)}, u32[]{:S(2)}) %collective-permute-start.3) | collective-permute-done | bytes 40992 | tf_op jit(solution)/shard_map/ppermute | solution.py:301
  52.1 0.3 send_kernel.1
  52.4 19.8 %all_to_all.15.images_ref = bf16[64,24,128]{2,1,0:T(8,128)(2,1)S(1)} all-to-all(bf16[64,24,128]{2,1,0:T(8,128)(2,1)S(1)} %get-tuple-element.26), channel_id=1, replica_groups=mesh['blk'=64,'probe'=4] {'blk'}, dimensions={0} | all-to-all | bytes 786432 | tf_op jit(solution)/shard_map/all_to_all | solution.py:305
  72.3 9.2 %second_kernel.1 = (f32[16,640]{1,0:T(8,128)S(1)}, f32[16,128]{1,0:T(8,128)S(1)}) custom-call(bf16[64,40,128]{2,1,0:T(8,128)(2,1)S(1)} %all-to-all-done.got_ref, bf16[64,24,128]{2,1,0:T(8,128)(2,1)S(1)} %all_to_all.15.images_ref, bf16[640,10240]{1,0:T(8,128)(2,1)S(1)} %get-tuple-element.27.tile_ref), custom_call_target="tpu_custom_call" | custom-call | tf_op jit(solution)/shard_map/second_kernel/pallas_call | solution.py:289
  81.5 0.0 collective-permute-start.4
  81.5 1.2 %collective-permute-done.4 = f32[16,640]{1,0:T(8,128)S(1)} collective-permute-done((f32[16,640]{1,0:T(8,128)S(1)}, f32[16,640]{1,0:T(8,128)S(1)}, u32[]{:S(2)}, u32[]{:S(2)}) %collective-permute-start.4) | collective-permute-done | bytes 40992 | tf_op jit(solution)/shard_map/ppermute | solution.py:301
  82.8 0.6 collective-permute-start.5
  83.4 4.9 %collective-permute-done.5.far_ref = f32[16,640]{1,0:T(8,128)S(1)} collective-permute-done((f32[16,640]{1,0:T(8,128)S(1)}, f32[16,640]{1,0:T(8,128)S(1)}, u32[]{:S(2)}, u32[]{:S(2)}) %collective-permute-start.5) | collective-permute-done | bytes 40992 | tf_op jit(solution)/shard_map/ppermute | solution.py:301
  88.3 0.3 sums_kernel.1
  88.5 17.8 %all_to_all.16.sums_ref = f32[64,8,128]{2,1,0:T(8,128)S(1)} all-to-all(f32[64,8,128]{2,1,0:T(8,128)S(1)} %get-tuple-element.30), channel_id=1, replica_groups=mesh['blk'=64,'probe'=4] {'blk'}, dimensions={0} | all-to-all | bytes 524288 | tf_op jit(solution)/shard_map/all_to_all | solution.py:305
  106.3 1.0 last_kernel.1
  107.3 0.1 slice.7
  107.4 0.1 slice.6
  107.5 0.1 copy.7
  107.6 0.1 copy.8
  107.7 0.6 pad_maximum_fusion
  (4 shorter events, 0.0 us)
Async XLA Ops:
  1.3 0.8 copy-start
  2.1 0.7 copy-start.1
  3.9 33.3 %all-to-all-start = ((bf16[64,40,128]{2,1,0:T(8,128)(2,1)}), bf16[64,40,128]{2,1,0:T(8,128)(2,1)S(1)}, u32[]{:S(2)}, u32[]{:S(2)}) async-start(bf16[64,40,128]{2,1,0:T(8,128)(2,1)} %get-tuple-element.23), calls=%async_computation | async-start | bytes 1310720 | tf_op jit(solution)/shard_map/all_to_all | solution.py:305
  16.5 1.3 %collective-permute-start = (f32[8,640]{1,0:T(8,128)S(1)}, f32[8,640]{1,0:T(8,128)S(1)}, u32[]{:S(2)}, u32[]{:S(2)}) collective-permute-start(f32[8,640]{1,0:T(8,128)S(1)} %get-tuple-element.22), channel_id=1, source_target_pairs={{0,1},{1,0},{2,3},{3,2},{4,5},{5,4},{6,7},{7,6},{8,9},{9,8},{10,11... | collective-permute-start | bytes 61448 | tf_op jit(solution)/shard_map/ppermute | solution.py:301
  17.8 5.6 %collective-permute-start.1 = (f32[8,640]{1,0:T(8,128)S(1)}, f32[8,640]{1,0:T(8,128)S(1)}, u32[]{:S(2)}, u32[]{:S(2)}) collective-permute-start(f32[8,640]{1,0:T(8,128)S(1)} %add.12), channel_id=1, source_target_pairs={{0,2},{1,3},{2,0},{3,1},{4,6},{5,7},{6,4},{7,5},{8,10},{9,11},{10,... | collective-permute-start | bytes 61448 | tf_op jit(solution)/shard_map/ppermute | solution.py:301
  45.4 1.2 %collective-permute-start.2 = (f32[16,640]{1,0:T(8,128)S(1)}, f32[16,640]{1,0:T(8,128)S(1)}, u32[]{:S(2)}, u32[]{:S(2)}) collective-permute-start(f32[16,640]{1,0:T(8,128)S(1)} %get-tuple-element.24), channel_id=1, source_target_pairs={{0,1},{1,0},{2,3},{3,2},{4,5},{5,4},{6,7},{7,6},{8,9},{9,8},{10,11... | collective-permute-start | bytes 122888 | tf_op jit(solution)/shard_map/ppermute | solution.py:301
  46.6 5.5 %collective-permute-start.3 = (f32[16,640]{1,0:T(8,128)S(1)}, f32[16,640]{1,0:T(8,128)S(1)}, u32[]{:S(2)}, u32[]{:S(2)}) collective-permute-start(f32[16,640]{1,0:T(8,128)S(1)} %add.14.near_ref), channel_id=1, source_target_pairs={{0,2},{1,3},{2,0},{3,1},{4,6},{5,7},{6,4},{7,5},{8,10},{9,11},{10,... | collective-permute-start | bytes 122888 | tf_op jit(solution)/shard_map/ppermute | solution.py:301
  81.5 1.2 %collective-permute-start.4 = (f32[16,640]{1,0:T(8,128)S(1)}, f32[16,640]{1,0:T(8,128)S(1)}, u32[]{:S(2)}, u32[]{:S(2)}) collective-permute-start(f32[16,640]{1,0:T(8,128)S(1)} %get-tuple-element.29), channel_id=1, source_target_pairs={{0,1},{1,0},{2,3},{3,2},{4,5},{5,4},{6,7},{7,6},{8,9},{9,8},{10,11... | collective-permute-start | bytes 122888 | tf_op jit(solution)/shard_map/ppermute | solution.py:301
  82.8 5.5 %collective-permute-start.5 = (f32[16,640]{1,0:T(8,128)S(1)}, f32[16,640]{1,0:T(8,128)S(1)}, u32[]{:S(2)}, u32[]{:S(2)}) collective-permute-start(f32[16,640]{1,0:T(8,128)S(1)} %add.15.near_ref), channel_id=1, source_target_pairs={{0,2},{1,3},{2,0},{3,1},{4,6},{5,7},{6,4},{7,5},{8,10},{9,11},{10,... | collective-permute-start | bytes 122888 | tf_op jit(solution)/shard_map/ppermute | solution.py:301

commit v3 on v2

v3 whole, which is shorter than its diff:
```python
import jax
import jax.numpy as jnp
from jax import lax
from jax.experimental import pallas as pl
from jax.experimental.pallas import tpu as pltpu
from jax.sharding import PartitionSpec as P

COLS = 16
FEAT = 8
LANES = 128
REST = 32
DEPTH = 48
WIDTH = 2560
LOG2E = 1.4426950408889634
LIMIT = 24 * 2**20


def rounded(value):
    return value.astype(jnp.bfloat16).astype(jnp.float32)


def split3(value):
    high = rounded(value)
    mid = rounded(value - high)
    return high, mid, value - high - mid


def norm_rows(points, ones_first):
    high, mid, low = split3((-0.5 * LOG2E) * jnp.sum(points * points, 0, keepdims=True))
    row = lax.broadcasted_iota(jnp.int32, points.shape, 0)
    at = 3 if ones_first else 0
    value = jnp.where(row == at, high, jnp.where(row == at + 1, mid, jnp.where(row == at + 2, low, 0.0)))
    other = (row < 3) if ones_first else ((row >= 3) & (row < 6))
    return jnp.where(other, 1.0, value)


def left_rows(high, low):
    return jnp.concatenate([high, high, high, low, low, norm_rows(high + low, True)], 0)


def right_rows(points):
    high = rounded(points)
    points = high + rounded(points - high)
    top, mid, end = split3(points * LOG2E)
    return jnp.concatenate([top, mid, end, top, mid, norm_rows(points, False)], 0)


def lane_of(shape):
    return lax.broadcasted_iota(jnp.int32, shape, len(shape) - 1)


def turn(value, by):
    by = by % value.shape[-1]
    return pltpu.roll(value, by, value.ndim - 1) if by else value


def pack_rest(groups):
    lane = lane_of((8, LANES))
    out = jnp.zeros((8, LANES), jnp.float32)
    for at, group in enumerate(groups):
        out = jnp.where((lane >= REST * at) & (lane < REST * (at + 1)), turn(group, REST * at), out)
    return out


def join_rest(parts, group):
    lane = lane_of((8, LANES))
    out = None
    for at, part in enumerate(parts):
        moved = turn(part, REST * (at - group))
        out = moved if out is None else jnp.where(lane >= REST * at, moved, out)
    return out


def repeat_piece(ref, piece):
    piece = piece.astype(ref.dtype)

    def put(block, carry):
        ref[block] = piece
        return carry

    lax.fori_loop(0, ref.shape[0], put, 0, unroll=8)


def pack_kernel(place_ref, points_hbm, targets_hbm, signs_hbm, piece_ref, mine_ref,
                points_ref, targets_ref, signs_ref, rhs_ref, wide_ref, sems):
    moves = [
        pltpu.make_async_copy(src, dst, sems.at[at])
        for at, (src, dst) in enumerate(
            ((points_hbm, points_ref), (targets_hbm, targets_ref), (signs_hbm, signs_ref))
        )
    ]
    for move in moves:
        move.start()
    for move in moves:
        move.wait()
    quarter = points_ref.shape[1]
    rhs_ref[0:1, :] = targets_ref[...][None, :]
    rhs_ref[1:COLS, :] = 2.0 * signs_ref[...].astype(jnp.float32) - 1.0
    wide_ref[:, 0:quarter] = points_ref[...]
    points = wide_ref[...]
    width = rhs_ref.shape[1]
    rhs = pltpu.roll(rhs_ref[...], lax.rem(width - place_ref[0] * quarter, width), 1)
    mine_ref[0:FEAT, :] = points_ref[...]
    mine_ref[FEAT : FEAT + COLS, :] = rhs[:, 0:quarter]
    high = rounded(points)
    low = rounded(points - high)
    ends = slice(LANES, 2 * LANES)
    rest = pack_rest([rhs[:8, ends], rhs[8:, ends], high[:, ends], low[:, ends]])
    repeat_piece(
        piece_ref, jnp.concatenate([high[:, :LANES], low[:, :LANES], rhs[:, :LANES], rest], 0)
    )


def tile_kernel(place_ref, near_ref, far_ref, got_ref, tile_ref, image_ref, sides_ref, left_ref, rhs_ref, wide_ref):
    place = place_ref[0]
    rows, quarter = near_ref.shape[0] // 2, near_ref.shape[1]
    wide_ref[...] = jnp.zeros_like(wide_ref)
    own = jnp.zeros(wide_ref.shape, jnp.float32)
    for flip in range(4):
        ref = near_ref if flip < 2 else far_ref
        first = rows * (flip % 2)
        wide_ref[:, 0:quarter] = ref[first : first + rows, :]
        own += pltpu.roll(wide_ref[...], jnp.bitwise_xor(place, flip) * quarter, 1)
    sides_ref[...] = own[FEAT:]
    right = right_rows(own[:FEAT]).astype(jnp.bfloat16)
    blocks = got_ref.shape[0]

    def left_and_rhs(block):
        if block < blocks:
            piece = got_ref[block].astype(jnp.float32)
            return left_rows(piece[0:8], piece[8:16]), piece[16:32]
        group = block - blocks
        parts = [got_ref[4 * group + q].astype(jnp.float32)[32:40] for q in range(4)]
        joined = [join_rest(parts, g) for g in range(4)]
        return left_rows(joined[2], joined[3]), jnp.concatenate(joined[:2], 0)

    total = jnp.zeros(image_ref.shape, jnp.float32)
    each = WIDTH // LANES
    for first in range(0, tile_ref.shape[0], WIDTH):
        for block in range(first // LANES, first // LANES + each):
            place = slice(block * LANES, (block + 1) * LANES)
            left, rhs = left_and_rhs(block)
            left_ref[place, :] = jnp.transpose(left).astype(jnp.bfloat16)
            rhs_ref[:, place] = rhs.astype(jnp.bfloat16)
        place = slice(first, first + WIDTH)
        power = jnp.dot(left_ref[place, :], right, preferred_element_type=jnp.float32)
        tile = jnp.exp2(power).astype(jnp.bfloat16)
        tile_ref[place, :] = tile
        total += jnp.dot(rhs_ref[:, place], tile, preferred_element_type=jnp.float32)
    image_ref[...] = total


def safe_ratio(top, bottom):
    good = bottom > 0.0
    return jnp.where(good, top / jnp.where(good, bottom, 1.0), 0.0)


def row_sum(value):
    return jnp.sum(value, 1, keepdims=True)


def send_kernel(place_ref, rhs_ref, near_ref, far_ref, piece_ref, image_ref):
    rhs = rhs_ref[...]
    image = near_ref[...] + far_ref[...] + 0.5 * rhs
    image_ref[...] = image
    norm, curv, quad = row_sum(rhs * rhs), row_sum(rhs * image), row_sum(image * image)
    best = safe_ratio(curv, quad)
    left = row_sum(jnp.square(rhs - best * image))
    share = safe_ratio(curv, norm)
    width = rhs.shape[1]
    back = lax.rem(width - place_ref[0] * (width // 4), width)
    rest = pltpu.roll(image - share * rhs, back, 1)
    packed = pack_rest([rest[:8, LANES : 2 * LANES], rest[8:, LANES : 2 * LANES]])
    lane = lane_of((8, LANES))
    at = 2 * REST
    for value in (norm, curv, quad, left, share, best):
        for part in split3(value):
            for half in (part[:8], part[8:]):
                packed = jnp.where(lane == at, half, packed)
                at += 1
    repeat_piece(piece_ref, jnp.concatenate([rest[:, :LANES], packed], 0))


def second_kernel(got_ref, images_ref, tile_ref, out_ref, coeff_ref, dir_ref, sums_ref):
    blocks = got_ref.shape[0]
    zero = jnp.zeros((8, LANES), jnp.float32)

    def add(block, total):
        value = images_ref[block].astype(jnp.float32)[16:24]
        value = value + turn(value, -2) + turn(value, -4)
        sums_ref[block] = value
        return total + value

    norm = lax.fori_loop(0, blocks, add, zero, unroll=16)
    step = norm / turn(norm, -6)

    def grow(block, total):
        value = sums_ref[block]
        gap = step - turn(value, -30)
        return total + turn(value, -18) + gap * gap * turn(value, -12)

    ratio = lax.fori_loop(0, blocks, grow, zero, unroll=16) / norm
    at = 2 * REST

    def column(value, at):
        return jnp.concatenate([value[:, at : at + 1], value[:, at + 1 : at + 2]], 0)

    step_col, ratio_col = column(step, at), column(ratio, at)
    lane = lane_of((COLS, LANES))
    coeff_ref[...] = jnp.where(lane == 0, step_col, jnp.where(lane == 1, ratio_col, 0.0))
    step_wide = jnp.broadcast_to(step_col, (COLS, LANES))
    grown = 1.0 + jnp.broadcast_to(ratio_col, (COLS, LANES))
    first = lane_of((8, LANES)) < REST
    step_rest = jnp.where(first, step_wide[:8], step_wide[8:])

    def put(value, block):
        dir_ref[:, block * LANES : (block + 1) * LANES] = value.astype(jnp.bfloat16)

    def product(first, width):
        return jnp.dot(
            dir_ref[:, first : first + width], tile_ref[first : first + width, :], preferred_element_type=jnp.float32
        )

    total = jnp.zeros(out_ref.shape, jnp.float32)
    for group in range(blocks // 4):
        ends = []
        for block in range(4 * group, 4 * group + 4):
            piece = got_ref[block].astype(jnp.float32)
            image = images_ref[block].astype(jnp.float32)
            scale = grown - step_wide * column(sums_ref[block], at + 24)
            put(scale * piece[16:32] - step_wide * image[:16], block)
            ends.append(jnp.where(first, scale[:8], scale[8:]) * piece[32:40] - step_rest * image[16:24])
        put(jnp.concatenate([join_rest(ends, 0), join_rest(ends, 1)], 0), blocks + group)
        if group % 4 == 3:
            total += product((group - 3) * 4 * LANES, 16 * LANES)
    out_ref[...] = total + product(blocks * LANES, blocks // 4 * LANES)


def sums_kernel(rhs_ref, image_ref, coeff_ref, near_ref, far_ref, piece_ref, res_ref, dir_ref, out_ref):
    rhs = rhs_ref[...]
    step, ratio = coeff_ref[:, 0:1], coeff_ref[:, 1:2]
    residual = rhs - step * image_ref[...]
    direction = residual + ratio * rhs
    image = near_ref[...] + far_ref[...] + 0.5 * direction
    res_ref[...], dir_ref[...], out_ref[...] = residual, direction, image
    quad = row_sum(image * image)
    best = safe_ratio(row_sum(residual * image), quad)
    left = row_sum(jnp.square(residual - best * image))
    values = (row_sum(residual * residual), row_sum(direction * image), quad, best, left)
    lane = lane_of((COLS, LANES))
    row = lax.broadcasted_iota(jnp.int32, (COLS, LANES), 0)
    piece = jnp.zeros((COLS, LANES), jnp.float32)
    for at, value in enumerate(values):
        piece = jnp.where(lane == row + COLS * at, value, piece)
    repeat_piece(piece_ref, jnp.sum(piece, 0, keepdims=True))


def last_kernel(place_ref, sums_ref, rhs_ref, res_ref, dir_ref, image_ref, coeff_ref,
                answer_ref, residual_ref, direction_ref, coeffs_ref):
    sums = sums_ref[:, 0, :]
    total = jnp.sum(sums, 0, keepdims=True)
    step_row = total / turn(total, -COLS)
    gap = step_row - turn(sums, -3 * COLS)
    grown = turn(sums, -4 * COLS) + gap * gap * turn(sums, -2 * COLS)
    ratio_row = jnp.sum(grown, 0, keepdims=True) / total
    lane = lane_of((COLS, LANES))
    row = lax.broadcasted_iota(jnp.int32, (COLS, LANES), 0)

    def column(value):
        return row_sum(jnp.where(lane == row, value, 0.0))

    step, ratio = column(step_row), column(ratio_row)
    first_step, first_ratio = coeff_ref[:, 0:1], coeff_ref[:, 1:2]
    direction = dir_ref[...]
    residual = res_ref[...] - step * image_ref[...]
    place = place_ref[0]

    def own_cols(value):
        out = value[0:4]
        for at in range(1, 4):
            out = jnp.where(place == at, value[4 * at : 4 * at + 4], out)
        return out

    answer_ref[...] = own_cols(first_step * rhs_ref[...] + step * direction)
    residual_ref[...] = own_cols(residual)
    direction_ref[...] = own_cols(residual + ratio * direction)
    for kind, values in enumerate(((first_step, step), (first_ratio, ratio))):
        for at, value in enumerate(values):
            picked = jnp.sum(jnp.where(lane == row - 4 * place, value, 0.0), 0, keepdims=True)
            coeffs_ref[kind, at : at + 1, :] = picked[:, 0:4]


VMEM = pl.BlockSpec(memory_space=pltpu.VMEM)
SMEM = pl.BlockSpec(memory_space=pltpu.SMEM)


def call(kernel, outs, scratch, *args, held=(), limit=LIMIT):
    kinds = [SMEM if a.shape == (1,) else pl.BlockSpec(memory_space=pltpu.HBM) if at in held else VMEM for at, a in enumerate(args)]
    return pl.pallas_call(
        kernel,
        out_shape=tuple(jax.ShapeDtypeStruct(shape, kind) for shape, kind in outs),
        in_specs=kinds,
        out_specs=tuple(VMEM for _ in outs),
        scratch_shapes=[pltpu.VMEM(*s) if isinstance(s, tuple) else s for s in scratch],
        compiler_params=pltpu.CompilerParams(vmem_limit_bytes=limit),
        name=kernel.__name__,
    )(*args)


def swap(value, bit):
    return lax.ppermute(value, "probe", [(i, i ^ bit) for i in range(4)])


def to_all_blocks(pieces):
    return lax.all_to_all(pieces, "blk", 0, 0)


def on_device(points, targets, signs):
    blocks = lax.axis_size("blk")
    rows = targets.shape[0]
    others = blocks * points.shape[1]
    place = lax.axis_index("probe").astype(jnp.int32)[None]
    f32, bf16 = jnp.float32, jnp.bfloat16
    wide = ((COLS, rows), f32)

    pieces, mine = call(
        pack_kernel,
        [((blocks, 40, LANES), bf16), ((FEAT + COLS, points.shape[1]), f32)],
        [
            (points.shape, f32), (targets.shape, f32), (signs.shape, signs.dtype), wide,
            ((FEAT, 2 * LANES), f32), pltpu.SemaphoreType.DMA((3,)),
        ],
        place, points, targets, signs,
        held=(1, 2, 3),
        limit=60 * 2**20,
    )
    got = to_all_blocks(pieces)
    near = jnp.concatenate([mine, swap(mine, 1)], 0)
    tile, part, rhs = call(
        tile_kernel,
        [((others, rows), bf16), wide, wide],
        [((others, DEPTH), bf16), ((COLS, others), bf16), ((FEAT + COLS, rows), f32)],
        place, near, swap(near, 2), got,
    )
    near = part + swap(part, 1)
    pieces, image = call(
        send_kernel, [((blocks, 24, LANES), bf16), wide], [], place, rhs, near, swap(near, 2)
    )
    images = to_all_blocks(pieces)
    part, coeff = call(
        second_kernel,
        [wide, ((COLS, LANES), f32)],
        [((COLS, others), bf16), ((blocks, 8, LANES), f32)],
        got, images, tile
    )
    near = part + swap(part, 1)
    pieces, residual, direction, image = call(
        sums_kernel, [((blocks, 1, LANES), f32), wide, wide, wide], [], rhs, image, coeff, near, swap(near, 2)
    )
    sums = to_all_blocks(pieces)
    small = ((4, rows), f32)
    answer, residual, direction, coeffs = call(
        last_kernel,
        [small, small, small, ((2, 2, 4), f32)],
        [],
        place, sums, rhs, residual, direction, image, coeff,
    )
    return (answer, residual, direction, coeffs)


def solution(mesh):
    placed = (P(None, ("blk", "probe")), P("blk"), P(None, "blk"))
    return jax.shard_map(
        on_device,
        mesh=mesh,
        in_specs=placed,
        out_specs=(P("probe", "blk"), P("probe", "blk"), P("probe", "blk"), P(None, None, "probe")),
        check_vma=False,
    )
```

time: 109 us -> 95.4 us (0.88)
  Pallas kernels: 20.1 us -> 11.9 us
  blocking collectives: 37.6 us -> 35.6 us
  local copies, waits for them, and re-layouts: 2.54 us -> 0.74 us
    pallas_call x6, Pallas kernels: 20.1 us -> 11.9 us  [call(): pl.pallas_call(kernel, out_shape=tuple((jax.ShapeDtypeStruct(shape, kind)...]
    all_to_all x2, blocking collectives: 37.6 us -> 35.6 us  [to_all_blocks(): return lax.all_to_all(pieces, 'blk', 0, 0)]
    all_to_all x1, waiting for transfers between devices: 13.8 us -> 12.4 us  [to_all_blocks(): return lax.all_to_all(pieces, 'blk', 0, 0)]
  transfers between devices with their start and end apart: 7 -> 7, of which waited for: 7 -> 7; matrix products, arithmetic and copies ran while one was open for 0% -> 1% of each run, Pallas kernels for 0% -> 0%
where the time goes in v3:
time: 95.4 us; the launch traced here: 95.1 us
  blocking collectives  35.6 us (37%)
  waiting for transfers between devices  31.4 us (33%)
  starting transfers between devices  14.8 us (16%)
  Pallas kernels  11.9 us (12%)
    all_to_all x2, blocking collectives, to_all_blocks(): return lax.all_to_all(pieces, 'blk', 0, 0)  35.6 us
    ppermute x6, waiting for transfers between devices, swap(): return lax.ppermute(value, 'probe', [(i, i ^ bit) for i in range(4)])  19 us
    all_to_all x1, starting transfers between devices, to_all_blocks(): return lax.all_to_all(pieces, 'blk', 0, 0)  12.7 us
    all_to_all x1, waiting for transfers between devices, to_all_blocks(): return lax.all_to_all(pieces, 'blk', 0, 0)  12.4 us
    pallas_call x6, Pallas kernels, call(): pl.pallas_call(kernel, out_shape=tuple((jax.ShapeDtypeStruct(shape, kind)...  11.9 us
    ppermute x6, starting transfers between devices, swap(): return lax.ppermute(value, 'probe', [(i, i ^ bit) for i in range(4)])  2.15 us
  transfers between devices with their start and end apart: 7, of which 7 were waited for; matrix products, arithmetic and copies ran while one was open for 1% of the time, Pallas kernels for 0%

profile of v3, /device:TPU:16, one launch (start us, length us, event | category | flops | bytes accessed | tf_op | source)
XLA Modules:
  0.0 95.1 jit_solution(8924785707504121914)
XLA Ops:
  0.6 1.9 %pack_kernel.1 = (bf16[64,40,128]{2,1,0:T(8,128)(2,1)}, f32[24,160]{1,0:T(8,128)}) custom-call(s32[1]{0:T(128)} %bitcast.place_ref, f32[8,160]{1,0:T(8,128)} %points_hbm.1, f32[640]{0:T(1024)} %targets_hbm.1, s32[15,640]{1,0:T(8,128)} %signs_hbm.1), custom_call_target="tpu_custom_call" | custom-call | tf_op jit(solution)/shard_map/pack_kernel/pallas_call | solution.py:299
  2.6 12.7 %all-to-all-start = ((bf16[64,40,128]{2,1,0:T(8,128)(2,1)}), bf16[64,40,128]{2,1,0:T(8,128)(2,1)S(1)}, u32[]{:S(2)}, u32[]{:S(2)}) async-start(bf16[64,40,128]{2,1,0:T(8,128)(2,1)} %get-tuple-element.18), calls=%async_computation | async-start | bytes 1310720 | tf_op jit(solution)/shard_map/all_to_all | solution.py:315
  15.2 0.1 collective-permute-start
  15.3 0.7 constant_dynamic-update-slice_fusion.1
  16.1 0.7 collective-permute-done
  16.7 0.6 collective-permute-start.1
  17.4 6.2 %collective-permute-done.1.far_ref = f32[48,160]{1,0:T(8,128)S(1)} collective-permute-done((f32[48,160]{1,0:T(8,128)S(1)}, f32[48,160]{1,0:T(8,128)S(1)}, u32[]{:S(2)}, u32[]{:S(2)}) %collective-permute-start.1) | collective-permute-done | bytes 30752 | tf_op jit(solution)/shard_map/ppermute | solution.py:311
  23.5 12.4 %all-to-all-done.got_ref = bf16[64,40,128]{2,1,0:T(8,128)(2,1)S(1)} async-done(((bf16[64,40,128]{2,1,0:T(8,128)(2,1)}), bf16[64,40,128]{2,1,0:T(8,128)(2,1)S(1)}, u32[]{:S(2)}, u32[]{:S(2)}) %all-to-all-start) | async-done | bytes 655392 | tf_op jit(solution)/shard_map/all_to_all | solution.py:315
  35.9 5.6 %tile_kernel.1 = (bf16[10240,640]{1,0:T(8,128)(2,1)S(1)}, f32[16,640]{1,0:T(8,128)S(1)}, f32[16,640]{1,0:T(8,128)S(1)}) custom-call(s32[1]{0:T(128)} %bitcast.place_ref, f32[48,160]{1,0:T(8,128)S(1)} %constant_dynamic-update-slice_fusion.near_ref, f32[48,160]{1,0:T(8,128)S(1)} %collective-permute-done.1.far_ref, bf16[64,40,128]{2,1,0:T(8,128)(2,1)S(1)} %all-to-all-done.got_ref), custom_call_target="tpu_custom_call" | custom-call | tf_op jit(solution)/shard_map/tile_kernel/pallas_call | solution.py:299
  41.5 0.1 collective-permute-start.2
  41.6 1.2 %collective-permute-done.2 = f32[16,640]{1,0:T(8,128)S(1)} collective-permute-done((f32[16,640]{1,0:T(8,128)S(1)}, f32[16,640]{1,0:T(8,128)S(1)}, u32[]{:S(2)}, u32[]{:S(2)}) %collective-permute-start.2) | collective-permute-done | bytes 40992 | tf_op jit(solution)/shard_map/ppermute | solution.py:311
  42.8 0.6 collective-permute-start.3
  43.5 4.9 %collective-permute-done.3.far_ref = f32[16,640]{1,0:T(8,128)S(1)} collective-permute-done((f32[16,640]{1,0:T(8,128)S(1)}, f32[16,640]{1,0:T(8,128)S(1)}, u32[]{:S(2)}, u32[]{:S(2)}) %collective-permute-start.3) | collective-permute-done | bytes 40992 | tf_op jit(solution)/shard_map/ppermute | solution.py:311
  48.4 0.3 send_kernel.1
  48.7 19.8 %all_to_all.15.images_ref = bf16[64,24,128]{2,1,0:T(8,128)(2,1)S(1)} all-to-all(bf16[64,24,128]{2,1,0:T(8,128)(2,1)S(1)} %get-tuple-element.22), channel_id=1, replica_groups=mesh['blk'=64,'probe'=4] {'blk'}, dimensions={0} | all-to-all | bytes 786432 | tf_op jit(solution)/shard_map/all_to_all | solution.py:315
  68.5 2.9 %second_kernel.1 = (f32[16,640]{1,0:T(8,128)S(1)}, f32[16,128]{1,0:T(8,128)S(1)}) custom-call(bf16[64,40,128]{2,1,0:T(8,128)(2,1)S(1)} %all-to-all-done.got_ref, bf16[64,24,128]{2,1,0:T(8,128)(2,1)S(1)} %all_to_all.15.images_ref, bf16[10240,640]{1,0:T(8,128)(2,1)S(1)} %get-tuple-element.23.tile_ref), custom_call_target="tpu_custom_call" | custom-call | tf_op jit(solution)/shard_map/second_kernel/pallas_call | solution.py:299
  71.4 0.1 collective-permute-start.4
  71.5 1.2 %collective-permute-done.4 = f32[16,640]{1,0:T(8,128)S(1)} collective-permute-done((f32[16,640]{1,0:T(8,128)S(1)}, f32[16,640]{1,0:T(8,128)S(1)}, u32[]{:S(2)}, u32[]{:S(2)}) %collective-permute-start.4) | collective-permute-done | bytes 40992 | tf_op jit(solution)/shard_map/ppermute | solution.py:311
  72.7 0.6 collective-permute-start.5
  73.3 4.9 %collective-permute-done.5.far_ref = f32[16,640]{1,0:T(8,128)S(1)} collective-permute-done((f32[16,640]{1,0:T(8,128)S(1)}, f32[16,640]{1,0:T(8,128)S(1)}, u32[]{:S(2)}, u32[]{:S(2)}) %collective-permute-start.5) | collective-permute-done | bytes 40992 | tf_op jit(solution)/shard_map/ppermute | solution.py:311
  78.2 0.3 sums_kernel.1
  78.5 15.8 %all_to_all.16.sums_ref = f32[64,1,128]{2,1,0:T(1,128)S(1)} all-to-all(f32[64,1,128]{2,1,0:T(1,128)S(1)} %get-tuple-element.26), channel_id=1, replica_groups=mesh['blk'=64,'probe'=4] {'blk'}, dimensions={0} | all-to-all | bytes 65536 | tf_op jit(solution)/shard_map/all_to_all | solution.py:315
  94.2 0.8 last_kernel.1
  (3 shorter events, 0.0 us)
Async XLA Ops:
  2.6 33.4 %all-to-all-start = ((bf16[64,40,128]{2,1,0:T(8,128)(2,1)}), bf16[64,40,128]{2,1,0:T(8,128)(2,1)S(1)}, u32[]{:S(2)}, u32[]{:S(2)}) async-start(bf16[64,40,128]{2,1,0:T(8,128)(2,1)} %get-tuple-element.18), calls=%async_computation | async-start | bytes 1310720 | tf_op jit(solution)/shard_map/all_to_all | solution.py:315
  15.2 1.5 %collective-permute-start = (f32[24,160]{1,0:T(8,128)}, f32[24,160]{1,0:T(8,128)S(1)}, u32[]{:S(2)}, u32[]{:S(2)}) collective-permute-start(f32[24,160]{1,0:T(8,128)} %get-tuple-element.17), channel_id=1, source_target_pairs={{0,1},{1,0},{2,3},{3,2},{4,5},{5,4},{6,7},{7,6},{8,9},{9,8},{10,11... | collective-permute-start | bytes 46088 | tf_op jit(solution)/shard_map/ppermute | solution.py:311
  16.7 6.8 %collective-permute-start.1 = (f32[48,160]{1,0:T(8,128)S(1)}, f32[48,160]{1,0:T(8,128)S(1)}, u32[]{:S(2)}, u32[]{:S(2)}) collective-permute-start(f32[48,160]{1,0:T(8,128)S(1)} %constant_dynamic-update-slice_fusion.near_ref), channel_id=1, source_target_pairs={{0,2},{1,3},{2,0},{3,1},{4,6},{5,7},{6,4},{7,5},{8,10},{9,11},{10,... | collective-permute-start | bytes 92168 | tf_op jit(solution)/shard_map/ppermute | solution.py:311
  41.5 1.3 %collective-permute-start.2 = (f32[16,640]{1,0:T(8,128)S(1)}, f32[16,640]{1,0:T(8,128)S(1)}, u32[]{:S(2)}, u32[]{:S(2)}) collective-permute-start(f32[16,640]{1,0:T(8,128)S(1)} %get-tuple-element.20), channel_id=1, source_target_pairs={{0,1},{1,0},{2,3},{3,2},{4,5},{5,4},{6,7},{7,6},{8,9},{9,8},{10,11... | collective-permute-start | bytes 122888 | tf_op jit(solution)/shard_map/ppermute | solution.py:311
  42.8 5.5 %collective-permute-start.3 = (f32[16,640]{1,0:T(8,128)S(1)}, f32[16,640]{1,0:T(8,128)S(1)}, u32[]{:S(2)}, u32[]{:S(2)}) collective-permute-start(f32[16,640]{1,0:T(8,128)S(1)} %add.6.near_ref), channel_id=1, source_target_pairs={{0,2},{1,3},{2,0},{3,1},{4,6},{5,7},{6,4},{7,5},{8,10},{9,11},{10,... | collective-permute-start | bytes 122888 | tf_op jit(solution)/shard_map/ppermute | solution.py:311
  71.4 1.3 %collective-permute-start.4 = (f32[16,640]{1,0:T(8,128)S(1)}, f32[16,640]{1,0:T(8,128)S(1)}, u32[]{:S(2)}, u32[]{:S(2)}) collective-permute-start(f32[16,640]{1,0:T(8,128)S(1)} %get-tuple-element.25), channel_id=1, source_target_pairs={{0,1},{1,0},{2,3},{3,2},{4,5},{5,4},{6,7},{7,6},{8,9},{9,8},{10,11... | collective-permute-start | bytes 122888 | tf_op jit(solution)/shard_map/ppermute | solution.py:311
  72.7 5.5 %collective-permute-start.5 = (f32[16,640]{1,0:T(8,128)S(1)}, f32[16,640]{1,0:T(8,128)S(1)}, u32[]{:S(2)}, u32[]{:S(2)}) collective-permute-start(f32[16,640]{1,0:T(8,128)S(1)} %add.7.near_ref), channel_id=1, source_target_pairs={{0,2},{1,3},{2,0},{3,1},{4,6},{5,7},{6,4},{7,5},{8,10},{9,11},{10,... | collective-permute-start | bytes 122888 | tf_op jit(solution)/shard_map/ppermute | solution.py:311

commit v4 on v3

--- a/solution.py
+++ b/solution.py
@@ -106,12 +106,16 @@
     low = rounded(points - high)
     ends = slice(LANES, 2 * LANES)
     rest = pack_rest([rhs[:8, ends], rhs[8:, ends], high[:, ends], low[:, ends]])
+    left = rhs[0:1] - rounded(rhs[0:1])
+    row = lax.broadcasted_iota(jnp.int32, (8, LANES), 0)
+    ends_left = jnp.where(lane_of((8, LANES)) < REST, left[:, ends], 0.0)
+    left = jnp.where(row == 0, left[:, :LANES], jnp.where(row == 1, ends_left, 0.0))
     repeat_piece(
-        piece_ref, jnp.concatenate([high[:, :LANES], low[:, :LANES], rhs[:, :LANES], rest], 0)
-    )
-
-
-def tile_kernel(place_ref, near_ref, far_ref, got_ref, tile_ref, image_ref, sides_ref, left_ref, rhs_ref, wide_ref):
+        piece_ref, jnp.concatenate([high[:, :LANES], low[:, :LANES], rhs[:, :LANES], rest, left], 0)
+    )
+
+
+def own_kernel(place_ref, near_ref, far_ref, right_ref, sides_ref, wide_ref):
     place = place_ref[0]
     rows, quarter = near_ref.shape[0] // 2, near_ref.shape[1]
     wide_ref[...] = jnp.zeros_like(wide_ref)
@@ -122,7 +126,11 @@
         wide_ref[:, 0:quarter] = ref[first : first + rows, :]
         own += pltpu.roll(wide_ref[...], jnp.bitwise_xor(place, flip) * quarter, 1)
     sides_ref[...] = own[FEAT:]
-    right = right_rows(own[:FEAT]).astype(jnp.bfloat16)
+    right_ref[...] = right_rows(own[:FEAT]).astype(jnp.bfloat16)
+
+
+def tile_kernel(right_ref, got_ref, tile_ref, image_ref, left_ref, rhs_ref):
+    right = right_ref[...]
     blocks = got_ref.shape[0]
 
     def left_and_rhs(block):
@@ -181,7 +189,14 @@
     repeat_piece(piece_ref, jnp.concatenate([rest[:, :LANES], packed], 0))
 
 
-def second_kernel(got_ref, images_ref, tile_ref, out_ref, coeff_ref, dir_ref, sums_ref):
+def cols_of(value, place):
+    out = value[0:4]
+    for at in range(1, 4):
+        out = jnp.where(place == at, value[4 * at : 4 * at + 4], out)
+    return out
+
+
+def second_kernel(place_ref, got_ref, images_ref, tile_ref, keep_ref, give_ref, coeff_ref, dir_ref, sums_ref):
     blocks = got_ref.shape[0]
     zero = jnp.zeros((8, LANES), jnp.float32)
 
@@ -213,6 +228,8 @@
     first = lane_of((8, LANES)) < REST
     step_rest = jnp.where(first, step_wide[:8], step_wide[8:])
 
+    top = lax.broadcasted_iota(jnp.int32, (COLS, LANES), 0) == 0
+
     def put(value, block):
         dir_ref[:, block * LANES : (block + 1) * LANES] = value.astype(jnp.bfloat16)
 
@@ -221,72 +238,71 @@
             dir_ref[:, first : first + width], tile_ref[first : first + width, :], preferred_element_type=jnp.float32
         )
 
-    total = jnp.zeros(out_ref.shape, jnp.float32)
+    total = jnp.zeros((COLS, keep_ref.shape[1]), jnp.float32)
     for group in range(blocks // 4):
         ends = []
         for block in range(4 * group, 4 * group + 4):
             piece = got_ref[block].astype(jnp.float32)
             image = images_ref[block].astype(jnp.float32)
             scale = grown - step_wide * column(sums_ref[block], at + 24)
-            put(scale * piece[16:32] - step_wide * image[:16], block)
-            ends.append(jnp.where(first, scale[:8], scale[8:]) * piece[32:40] - step_rest * image[16:24])
+            main = piece[16:32] + jnp.where(top, piece[40:41], 0.0)
+            ends_rhs = piece[32:40] + jnp.where(top[:8], piece[41:42], 0.0)
+            put(scale * main - step_wide * image[:16], block)
+            ends.append(jnp.where(first, scale[:8], scale[8:]) * ends_rhs - step_rest * image[16:24])
         put(jnp.concatenate([join_rest(ends, 0), join_rest(ends, 1)], 0), blocks + group)
-        if group % 4 == 3:
-            total += product((group - 3) * 4 * LANES, 16 * LANES)
-    out_ref[...] = total + product(blocks * LANES, blocks // 4 * LANES)
-
-
-def sums_kernel(rhs_ref, image_ref, coeff_ref, near_ref, far_ref, piece_ref, res_ref, dir_ref, out_ref):
-    rhs = rhs_ref[...]
-    step, ratio = coeff_ref[:, 0:1], coeff_ref[:, 1:2]
-    residual = rhs - step * image_ref[...]
-    direction = residual + ratio * rhs
-    image = near_ref[...] + far_ref[...] + 0.5 * direction
+        if group % 2 == 1:
+            total += product((group - 1) * 4 * LANES, 8 * LANES)
+    total += product(blocks * LANES, blocks // 4 * LANES)
+    core = lax.rem(place_ref[0], 2)
+    for ref, at in ((keep_ref, core), (give_ref, 1 - core)):
+        ref[0:4, :], ref[4:8, :] = cols_of(total, at), cols_of(total, at + 2)
+
+
+def sums_kernel(place_ref, rhs_ref, image_ref, coeff_ref, near_ref, far_ref,
+                piece_ref, right_ref, res_ref, dir_ref, out_ref, steps_ref):
+    place = place_ref[0]
+    rhs, steps = cols_of(rhs_ref[...], place), cols_of(coeff_ref[...], place)
+    residual = rhs - steps[:, 0:1] * cols_of(image_ref[...], place)
+    direction = residual + steps[:, 1:2] * rhs
+    image = jnp.where(place < 2, near_ref[0:4, :], near_ref[4:8, :]) + far_ref[...] + 0.5 * direction
+    right_ref[...], steps_ref[...] = rhs, steps
     res_ref[...], dir_ref[...], out_ref[...] = residual, direction, image
     quad = row_sum(image * image)
     best = safe_ratio(row_sum(residual * image), quad)
     left = row_sum(jnp.square(residual - best * image))
     values = (row_sum(residual * residual), row_sum(direction * image), quad, best, left)
-    lane = lane_of((COLS, LANES))
-    row = lax.broadcasted_iota(jnp.int32, (COLS, LANES), 0)
-    piece = jnp.zeros((COLS, LANES), jnp.float32)
+    lane = lane_of((4, LANES))
+    row = lax.broadcasted_iota(jnp.int32, (4, LANES), 0)
+    piece = jnp.zeros((4, LANES), jnp.float32)
     for at, value in enumerate(values):
-        piece = jnp.where(lane == row + COLS * at, value, piece)
+        piece = jnp.where(lane == row + 4 * at, value, piece)
     repeat_piece(piece_ref, jnp.sum(piece, 0, keepdims=True))
 
 
-def last_kernel(place_ref, sums_ref, rhs_ref, res_ref, dir_ref, image_ref, coeff_ref,
+def last_kernel(sums_ref, right_ref, res_ref, dir_ref, image_ref, steps_ref,
                 answer_ref, residual_ref, direction_ref, coeffs_ref):
     sums = sums_ref[:, 0, :]
     total = jnp.sum(sums, 0, keepdims=True)
-    step_row = total / turn(total, -COLS)
-    gap = step_row - turn(sums, -3 * COLS)
-    grown = turn(sums, -4 * COLS) + gap * gap * turn(sums, -2 * COLS)
+    step_row = total / turn(total, -4)
+    gap = step_row - turn(sums, -12)
+    grown = turn(sums, -16) + gap * gap * turn(sums, -8)
     ratio_row = jnp.sum(grown, 0, keepdims=True) / total
-    lane = lane_of((COLS, LANES))
-    row = lax.broadcasted_iota(jnp.int32, (COLS, LANES), 0)
+    lane = lane_of((4, LANES))
+    row = lax.broadcasted_iota(jnp.int32, (4, LANES), 0)
 
     def column(value):
         return row_sum(jnp.where(lane == row, value, 0.0))
 
     step, ratio = column(step_row), column(ratio_row)
-    first_step, first_ratio = coeff_ref[:, 0:1], coeff_ref[:, 1:2]
+    first_step, first_ratio = steps_ref[:, 0:1], steps_ref[:, 1:2]
     direction = dir_ref[...]
     residual = res_ref[...] - step * image_ref[...]
-    place = place_ref[0]
-
-    def own_cols(value):
-        out = value[0:4]
-        for at in range(1, 4):
-            out = jnp.where(place == at, value[4 * at : 4 * at + 4], out)
-        return out
-
-    answer_ref[...] = own_cols(first_step * rhs_ref[...] + step * direction)
-    residual_ref[...] = own_cols(residual)
-    direction_ref[...] = own_cols(residual + ratio * direction)
+    answer_ref[...] = first_step * right_ref[...] + step * direction
+    residual_ref[...] = residual
+    direction_ref[...] = residual + ratio * direction
     for kind, values in enumerate(((first_step, step), (first_ratio, ratio))):
         for at, value in enumerate(values):
-            picked = jnp.sum(jnp.where(lane == row - 4 * place, value, 0.0), 0, keepdims=True)
+            picked = jnp.sum(jnp.where(lane == row, value, 0.0), 0, keepdims=True)
             coeffs_ref[kind, at : at + 1, :] = picked[:, 0:4]
 
 
@@ -325,7 +341,7 @@
 
     pieces, mine = call(
         pack_kernel,
-        [((blocks, 40, LANES), bf16), ((FEAT + COLS, points.shape[1]), f32)],
+        [((blocks, 48, LANES), bf16), ((FEAT + COLS, points.shape[1]), f32)],
         [
             (points.shape, f32), (targets.shape, f32), (signs.shape, signs.dtype), wide,
             ((FEAT, 2 * LANES), f32), pltpu.SemaphoreType.DMA((3,)),
@@ -336,34 +352,41 @@
     )
     got = to_all_blocks(pieces)
     near = jnp.concatenate([mine, swap(mine, 1)], 0)
-    tile, part, rhs = call(
+    right, rhs = call(
+        own_kernel, [((DEPTH, rows), bf16), wide], [((FEAT + COLS, rows), f32)], place, near, swap(near, 2)
+    )
+    tile, part = call(
         tile_kernel,
-        [((others, rows), bf16), wide, wide],
-        [((others, DEPTH), bf16), ((COLS, others), bf16), ((FEAT + COLS, rows), f32)],
-        place, near, swap(near, 2), got,
+        [((others, rows), bf16), wide],
+        [((others, DEPTH), bf16), ((COLS, others), bf16)],
+        right, got,
     )
     near = part + swap(part, 1)
     pieces, image = call(
-        send_kernel, [((blocks, 24, LANES), bf16), wide], [], place, rhs, near, swap(near, 2)
+        send_kernel, [((blocks, 24, LANES), f32), wide], [], place, rhs, near, swap(near, 2)
     )
     images = to_all_blocks(pieces)
-    part, coeff = call(
+    keep, give, coeff = call(
         second_kernel,
-        [wide, ((COLS, LANES), f32)],
+        [((8, rows), f32), ((8, rows), f32), ((COLS, LANES), f32)],
         [((COLS, others), bf16), ((blocks, 8, LANES), f32)],
-        got, images, tile
-    )
-    near = part + swap(part, 1)
-    pieces, residual, direction, image = call(
-        sums_kernel, [((blocks, 1, LANES), f32), wide, wide, wide], [], rhs, image, coeff, near, swap(near, 2)
+        place, got, images, tile,
+    )
+    near = keep + swap(give, 1)
+    far = swap(jnp.where(place[0] < 2, near[4:], near[:4]), 2)
+    small = ((4, rows), f32)
+    pieces, rhs, residual, direction, image, steps = call(
+        sums_kernel,
+        [((blocks, 1, LANES), f32), small, small, small, small, ((4, LANES), f32)],
+        [],
+        place, rhs, image, coeff, near, far,
     )
     sums = to_all_blocks(pieces)
-    small = ((4, rows), f32)
     answer, residual, direction, coeffs = call(
         last_kernel,
         [small, small, small, ((2, 2, 4), f32)],
         [],
-        place, sums, rhs, residual, direction, image, coeff,
+        sums, rhs, residual, direction, image, steps,
     )
     return (answer, residual, direction, coeffs)
 

time: 95.4 us -> 107 us (1.12)
  blocking collectives: 35.6 us -> 44.4 us
  waiting for transfers between devices: 31.4 us -> 33.2 us
    all_to_all x2, blocking collectives: 35.6 us -> 44.4 us  [to_all_blocks(): return lax.all_to_all(pieces, 'blk', 0, 0)]
    all_to_all x1, waiting for transfers between devices: 12.4 us -> 14.7 us  [to_all_blocks(): return lax.all_to_all(pieces, 'blk', 0, 0)]
    pallas_call x6 -> x7, Pallas kernels: 11.9 us -> 12.2 us  [call(): pl.pallas_call(kernel, out_shape=tuple((jax.ShapeDtypeStruct(shape, kind)...]
where the time goes in v4:
time: 107 us; the launch traced here: 106 us
  blocking collectives  44.4 us (41%)
  waiting for transfers between devices  33.2 us (31%)
  starting transfers between devices  14.9 us (14%)
  Pallas kernels  12.2 us (11%)
    all_to_all x2, blocking collectives, to_all_blocks(): return lax.all_to_all(pieces, 'blk', 0, 0)  44.4 us
    ppermute x6, waiting for transfers between devices, swap(): return lax.ppermute(value, 'probe', [(i, i ^ bit) for i in range(4)])  18.5 us
    all_to_all x1, waiting for transfers between devices, to_all_blocks(): return lax.all_to_all(pieces, 'blk', 0, 0)  14.7 us
    all_to_all x1, starting transfers between devices, to_all_blocks(): return lax.all_to_all(pieces, 'blk', 0, 0)  12.7 us
    pallas_call x7, Pallas kernels, call(): pl.pallas_call(kernel, out_shape=tuple((jax.ShapeDtypeStruct(shape, kind)...  12.2 us
    ppermute x6, starting transfers between devices, swap(): return lax.ppermute(value, 'probe', [(i, i ^ bit) for i in range(4)])  2.24 us
  transfers between devices with their start and end apart: 7, of which 7 were waited for; matrix products, arithmetic and copies ran while one was open for 1% of the time, Pallas kernels for 0%

profile of v4, /device:TPU:16, one launch (start us, length us, event | category | flops | bytes accessed | tf_op | source)
XLA Modules:
  0.0 106.2 jit_solution(6468670808510354737)
XLA Ops:
  0.6 2.0 %pack_kernel.1 = (bf16[64,48,128]{2,1,0:T(8,128)(2,1)}, f32[24,160]{1,0:T(8,128)}) custom-call(s32[1]{0:T(128)} %bitcast.place_ref, f32[8,160]{1,0:T(8,128)} %points_hbm.1, f32[640]{0:T(1024)} %targets_hbm.1, s32[15,640]{1,0:T(8,128)} %signs_hbm.1), custom_call_target="tpu_custom_call" | custom-call | tf_op jit(solution)/shard_map/pack_kernel/pallas_call | solution.py:315
  2.6 12.7 %all-to-all-start = ((bf16[64,48,128]{2,1,0:T(8,128)(2,1)}), bf16[64,48,128]{2,1,0:T(8,128)(2,1)S(1)}, u32[]{:S(2)}, u32[]{:S(2)}) async-start(bf16[64,48,128]{2,1,0:T(8,128)(2,1)} %get-tuple-element.24), calls=%async_computation | async-start | bytes 1572864 | tf_op jit(solution)/shard_map/all_to_all | solution.py:331
  15.3 0.1 collective-permute-start
  15.4 0.7 constant_dynamic-update-slice_fusion.1
  16.1 0.7 collective-permute-done
  16.8 0.6 collective-permute-start.1
  17.4 6.0 %collective-permute-done.1.far_ref = f32[48,160]{1,0:T(8,128)S(1)} collective-permute-done((f32[48,160]{1,0:T(8,128)S(1)}, f32[48,160]{1,0:T(8,128)S(1)}, u32[]{:S(2)}, u32[]{:S(2)}) %collective-permute-start.1) | collective-permute-done | bytes 30752 | tf_op jit(solution)/shard_map/ppermute | solution.py:327
  23.4 0.2 own_kernel.1
  23.6 14.7 %all-to-all-done.got_ref = bf16[64,48,128]{2,1,0:T(8,128)(2,1)S(1)} async-done(((bf16[64,48,128]{2,1,0:T(8,128)(2,1)}), bf16[64,48,128]{2,1,0:T(8,128)(2,1)S(1)}, u32[]{:S(2)}, u32[]{:S(2)}) %all-to-all-start) | async-done | bytes 786464 | tf_op jit(solution)/shard_map/all_to_all | solution.py:331
  38.3 5.6 %tile_kernel.1 = (bf16[10240,640]{1,0:T(8,128)(2,1)S(1)}, f32[16,640]{1,0:T(8,128)S(1)}) custom-call(bf16[48,640]{1,0:T(8,128)(2,1)S(1)} %get-tuple-element.23.right_ref, bf16[64,48,128]{2,1,0:T(8,128)(2,1)S(1)} %all-to-all-done.got_ref), custom_call_target="tpu_custom_call" | custom-call | tf_op jit(solution)/shard_map/tile_kernel/pallas_call | solution.py:315
  43.9 0.1 collective-permute-start.2
  44.0 1.2 %collective-permute-done.2 = f32[16,640]{1,0:T(8,128)S(1)} collective-permute-done((f32[16,640]{1,0:T(8,128)S(1)}, f32[16,640]{1,0:T(8,128)S(1)}, u32[]{:S(2)}, u32[]{:S(2)}) %collective-permute-start.2) | collective-permute-done | bytes 40992 | tf_op jit(solution)/shard_map/ppermute | solution.py:327
  45.2 0.6 collective-permute-start.3
  45.9 4.9 %collective-permute-done.3.far_ref = f32[16,640]{1,0:T(8,128)S(1)} collective-permute-done((f32[16,640]{1,0:T(8,128)S(1)}, f32[16,640]{1,0:T(8,128)S(1)}, u32[]{:S(2)}, u32[]{:S(2)}) %collective-permute-start.3) | collective-permute-done | bytes 40992 | tf_op jit(solution)/shard_map/ppermute | solution.py:327
  50.8 0.3 send_kernel.1
  51.1 28.5 %all_to_all.15.images_ref = f32[64,24,128]{2,1,0:T(8,128)S(1)} all-to-all(f32[64,24,128]{2,1,0:T(8,128)S(1)} %get-tuple-element.27), channel_id=1, replica_groups=mesh['blk'=64,'probe'=4] {'blk'}, dimensions={0} | all-to-all | bytes 1572864 | tf_op jit(solution)/shard_map/all_to_all | solution.py:331
  79.6 2.9 %second_kernel.1 = (f32[8,640]{1,0:T(8,128)S(1)}, f32[8,640]{1,0:T(8,128)S(1)}, f32[16,128]{1,0:T(8,128)S(1)}) custom-call(s32[1]{0:T(128)} %bitcast.place_ref, bf16[64,48,128]{2,1,0:T(8,128)(2,1)S(1)} %all-to-all-done.got_ref, f32[64,24,128]{2,1,0:T(8,128)S(1)} %all_to_all.15.images_ref, bf16[10240,640]{1,0:T(8,128)(2,1)S(1)} %get-tuple-element.28.tile_ref), custom_call_target="tpu_custom_call" | custom-call | tf_op jit(solution)/shard_map/second_kernel/pallas_call | solution.py:315
  82.6 0.1 collective-permute-start.4
  82.7 1.2 %collective-permute-done.4 = f32[8,640]{1,0:T(8,128)S(1)} collective-permute-done((f32[8,640]{1,0:T(8,128)S(1)}, f32[8,640]{1,0:T(8,128)S(1)}, u32[]{:S(2)}, u32[]{:S(2)}) %collective-permute-start.4) | collective-permute-done | bytes 20512 | tf_op jit(solution)/shard_map/ppermute | solution.py:327
  83.8 0.7 collective-permute-start.5
  84.6 4.5 %collective-permute-done.5.far_ref = f32[4,640]{1,0:T(4,128)S(1)} collective-permute-done((f32[4,640]{1,0:T(4,128)S(1)}, f32[4,640]{1,0:T(4,128)S(1)}, u32[]{:S(2)}, u32[]{:S(2)}) %collective-permute-start.5) | collective-permute-done | bytes 10272 | tf_op jit(solution)/shard_map/ppermute | solution.py:327
  89.1 0.4 sums_kernel.1
  89.5 15.9 %all_to_all.16.sums_ref = f32[64,1,128]{2,1,0:T(1,128)S(1)} all-to-all(f32[64,1,128]{2,1,0:T(1,128)S(1)} %get-tuple-element.32), channel_id=1, replica_groups=mesh['blk'=64,'probe'=4] {'blk'}, dimensions={0} | all-to-all | bytes 65536 | tf_op jit(solution)/shard_map/all_to_all | solution.py:331
  105.4 0.8 last_kernel.1
  (4 shorter events, 0.0 us)
Async XLA Ops:
  2.6 35.7 %all-to-all-start = ((bf16[64,48,128]{2,1,0:T(8,128)(2,1)}), bf16[64,48,128]{2,1,0:T(8,128)(2,1)S(1)}, u32[]{:S(2)}, u32[]{:S(2)}) async-start(bf16[64,48,128]{2,1,0:T(8,128)(2,1)} %get-tuple-element.24), calls=%async_computation | async-start | bytes 1572864 | tf_op jit(solution)/shard_map/all_to_all | solution.py:331
  15.3 1.5 %collective-permute-start = (f32[24,160]{1,0:T(8,128)}, f32[24,160]{1,0:T(8,128)S(1)}, u32[]{:S(2)}, u32[]{:S(2)}) collective-permute-start(f32[24,160]{1,0:T(8,128)} %get-tuple-element.21), channel_id=1, source_target_pairs={{0,1},{1,0},{2,3},{3,2},{4,5},{5,4},{6,7},{7,6},{8,9},{9,8},{10,11... | collective-permute-start | bytes 46088 | tf_op jit(solution)/shard_map/ppermute | solution.py:327
  16.8 6.6 %collective-permute-start.1 = (f32[48,160]{1,0:T(8,128)S(1)}, f32[48,160]{1,0:T(8,128)S(1)}, u32[]{:S(2)}, u32[]{:S(2)}) collective-permute-start(f32[48,160]{1,0:T(8,128)S(1)} %constant_dynamic-update-slice_fusion.near_ref), channel_id=1, source_target_pairs={{0,2},{1,3},{2,0},{3,1},{4,6},{5,7},{6,4},{7,5},{8,10},{9,11},{10,... | collective-permute-start | bytes 92168 | tf_op jit(solution)/shard_map/ppermute | solution.py:327
  43.9 1.3 %collective-permute-start.2 = (f32[16,640]{1,0:T(8,128)S(1)}, f32[16,640]{1,0:T(8,128)S(1)}, u32[]{:S(2)}, u32[]{:S(2)}) collective-permute-start(f32[16,640]{1,0:T(8,128)S(1)} %get-tuple-element.25), channel_id=1, source_target_pairs={{0,1},{1,0},{2,3},{3,2},{4,5},{5,4},{6,7},{7,6},{8,9},{9,8},{10,11... | collective-permute-start | bytes 122888 | tf_op jit(solution)/shard_map/ppermute | solution.py:327
  45.2 5.5 %collective-permute-start.3 = (f32[16,640]{1,0:T(8,128)S(1)}, f32[16,640]{1,0:T(8,128)S(1)}, u32[]{:S(2)}, u32[]{:S(2)}) collective-permute-start(f32[16,640]{1,0:T(8,128)S(1)} %add.6.near_ref), channel_id=1, source_target_pairs={{0,2},{1,3},{2,0},{3,1},{4,6},{5,7},{6,4},{7,5},{8,10},{9,11},{10,... | collective-permute-start | bytes 122888 | tf_op jit(solution)/shard_map/ppermute | solution.py:327
  82.6 1.3 %collective-permute-start.4 = (f32[8,640]{1,0:T(8,128)S(1)}, f32[8,640]{1,0:T(8,128)S(1)}, u32[]{:S(2)}, u32[]{:S(2)}) collective-permute-start(f32[8,640]{1,0:T(8,128)S(1)} %get-tuple-element.31), channel_id=1, source_target_pairs={{0,1},{1,0},{2,3},{3,2},{4,5},{5,4},{6,7},{7,6},{8,9},{9,8},{10,11... | collective-permute-start | bytes 61448 | tf_op jit(solution)/shard_map/ppermute | solution.py:327
  83.8 5.3 %collective-permute-start.5 = (f32[4,640]{1,0:T(4,128)S(1)}, f32[4,640]{1,0:T(4,128)S(1)}, u32[]{:S(2)}, u32[]{:S(2)}) collective-permute-start(f32[4,640]{1,0:T(4,128)S(1)} %slice_select_fusion), channel_id=1, source_target_pairs={{0,2},{1,3},{2,0},{3,1},{4,6},{5,7},{6,4},{7,5},{8,10},{9,11},{10,... | collective-permute-start | bytes 30728 | tf_op jit(solution)/shard_map/ppermute | solution.py:327

commit v5 on v4

--- a/solution.py
+++ b/solution.py
@@ -186,7 +186,8 @@
             for half in (part[:8], part[8:]):
                 packed = jnp.where(lane == at, half, packed)
                 at += 1
-    repeat_piece(piece_ref, jnp.concatenate([rest[:, :LANES], packed], 0))
+    piece = jnp.concatenate([rest[:, :LANES], packed], 0)
+    repeat_piece(piece_ref, jnp.concatenate([rounded(piece), piece - rounded(piece)], 0))
 
 
 def cols_of(value, place):
@@ -244,6 +245,7 @@
         for block in range(4 * group, 4 * group + 4):
             piece = got_ref[block].astype(jnp.float32)
             image = images_ref[block].astype(jnp.float32)
+            image = image[:24] + image[24:]
             scale = grown - step_wide * column(sums_ref[block], at + 24)
             main = piece[16:32] + jnp.where(top, piece[40:41], 0.0)
             ends_rhs = piece[32:40] + jnp.where(top[:8], piece[41:42], 0.0)
@@ -363,7 +365,7 @@
     )
     near = part + swap(part, 1)
     pieces, image = call(
-        send_kernel, [((blocks, 24, LANES), f32), wide], [], place, rhs, near, swap(near, 2)
+        send_kernel, [((blocks, 48, LANES), bf16), wide], [], place, rhs, near, swap(near, 2)
     )
     images = to_all_blocks(pieces)
     keep, give, coeff = call(

time: 107 us -> 107 us (level)
  no operation moved by 1% of the time
where the time goes in v5:
time: 107 us; the launch traced here: 106 us
  blocking collectives  44.4 us (41%)
  waiting for transfers between devices  33.2 us (31%)
  starting transfers between devices  14.9 us (14%)
  Pallas kernels  12.1 us (11%)
    all_to_all x2, blocking collectives, to_all_blocks(): return lax.all_to_all(pieces, 'blk', 0, 0)  44.4 us
    ppermute x6, waiting for transfers between devices, swap(): return lax.ppermute(value, 'probe', [(i, i ^ bit) for i in range(4)])  18.5 us
    all_to_all x1, waiting for transfers between devices, to_all_blocks(): return lax.all_to_all(pieces, 'blk', 0, 0)  14.7 us
    all_to_all x1, starting transfers between devices, to_all_blocks(): return lax.all_to_all(pieces, 'blk', 0, 0)  12.7 us
    pallas_call x7, Pallas kernels, call(): pl.pallas_call(kernel, out_shape=tuple((jax.ShapeDtypeStruct(shape, kind)...  12.1 us
    ppermute x6, starting transfers between devices, swap(): return lax.ppermute(value, 'probe', [(i, i ^ bit) for i in range(4)])  2.24 us
  transfers between devices with their start and end apart: 7, of which 7 were waited for; matrix products, arithmetic and copies ran while one was open for 1% of the time, Pallas kernels for 0%

profile of v5, /device:TPU:16, one launch (start us, length us, event | category | flops | bytes accessed | tf_op | source)
XLA Modules:
  0.0 106.2 jit_solution(4556081774491742849)
XLA Ops:
  0.6 2.0 %pack_kernel.1 = (bf16[64,48,128]{2,1,0:T(8,128)(2,1)}, f32[24,160]{1,0:T(8,128)}) custom-call(s32[1]{0:T(128)} %bitcast.place_ref, f32[8,160]{1,0:T(8,128)} %points_hbm.1, f32[640]{0:T(1024)} %targets_hbm.1, s32[15,640]{1,0:T(8,128)} %signs_hbm.1), custom_call_target="tpu_custom_call" | custom-call | tf_op jit(solution)/shard_map/pack_kernel/pallas_call | solution.py:317
  2.6 12.7 %all-to-all-start = ((bf16[64,48,128]{2,1,0:T(8,128)(2,1)}), bf16[64,48,128]{2,1,0:T(8,128)(2,1)S(1)}, u32[]{:S(2)}, u32[]{:S(2)}) async-start(bf16[64,48,128]{2,1,0:T(8,128)(2,1)} %get-tuple-element.24), calls=%async_computation | async-start | bytes 1572864 | tf_op jit(solution)/shard_map/all_to_all | solution.py:333
  15.3 0.1 collective-permute-start
  15.4 0.7 constant_dynamic-update-slice_fusion.1
  16.1 0.7 collective-permute-done
  16.8 0.6 collective-permute-start.1
  17.4 6.0 %collective-permute-done.1.far_ref = f32[48,160]{1,0:T(8,128)S(1)} collective-permute-done((f32[48,160]{1,0:T(8,128)S(1)}, f32[48,160]{1,0:T(8,128)S(1)}, u32[]{:S(2)}, u32[]{:S(2)}) %collective-permute-start.1) | collective-permute-done | bytes 30752 | tf_op jit(solution)/shard_map/ppermute | solution.py:329
  23.4 0.2 own_kernel.1
  23.6 14.7 %all-to-all-done.got_ref = bf16[64,48,128]{2,1,0:T(8,128)(2,1)S(1)} async-done(((bf16[64,48,128]{2,1,0:T(8,128)(2,1)}), bf16[64,48,128]{2,1,0:T(8,128)(2,1)S(1)}, u32[]{:S(2)}, u32[]{:S(2)}) %all-to-all-start) | async-done | bytes 786464 | tf_op jit(solution)/shard_map/all_to_all | solution.py:333
  38.3 5.6 %tile_kernel.1 = (bf16[10240,640]{1,0:T(8,128)(2,1)S(1)}, f32[16,640]{1,0:T(8,128)S(1)}) custom-call(bf16[48,640]{1,0:T(8,128)(2,1)S(1)} %get-tuple-element.23.right_ref, bf16[64,48,128]{2,1,0:T(8,128)(2,1)S(1)} %all-to-all-done.got_ref), custom_call_target="tpu_custom_call" | custom-call | tf_op jit(solution)/shard_map/tile_kernel/pallas_call | solution.py:317
  43.9 0.1 collective-permute-start.2
  44.0 1.2 %collective-permute-done.2 = f32[16,640]{1,0:T(8,128)S(1)} collective-permute-done((f32[16,640]{1,0:T(8,128)S(1)}, f32[16,640]{1,0:T(8,128)S(1)}, u32[]{:S(2)}, u32[]{:S(2)}) %collective-permute-start.2) | collective-permute-done | bytes 40992 | tf_op jit(solution)/shard_map/ppermute | solution.py:329
  45.2 0.6 collective-permute-start.3
  45.9 4.9 %collective-permute-done.3.far_ref = f32[16,640]{1,0:T(8,128)S(1)} collective-permute-done((f32[16,640]{1,0:T(8,128)S(1)}, f32[16,640]{1,0:T(8,128)S(1)}, u32[]{:S(2)}, u32[]{:S(2)}) %collective-permute-start.3) | collective-permute-done | bytes 40992 | tf_op jit(solution)/shard_map/ppermute | solution.py:329
  50.8 0.3 send_kernel.1
  51.1 28.5 %all_to_all.15.images_ref = bf16[64,48,128]{2,1,0:T(8,128)(2,1)S(1)} all-to-all(bf16[64,48,128]{2,1,0:T(8,128)(2,1)S(1)} %get-tuple-element.27), channel_id=1, replica_groups=mesh['blk'=64,'probe'=4] {'blk'}, dimensions={0} | all-to-all | bytes 1572864 | tf_op jit(solution)/shard_map/all_to_all | solution.py:333
  79.6 2.9 %second_kernel.1 = (f32[8,640]{1,0:T(8,128)S(1)}, f32[8,640]{1,0:T(8,128)S(1)}, f32[16,128]{1,0:T(8,128)S(1)}) custom-call(s32[1]{0:T(128)} %bitcast.place_ref, bf16[64,48,128]{2,1,0:T(8,128)(2,1)S(1)} %all-to-all-done.got_ref, bf16[64,48,128]{2,1,0:T(8,128)(2,1)S(1)} %all_to_all.15.images_ref, bf16[10240,640]{1,0:T(8,128)(2,1)S(1)} %get-tuple-element.28.tile_ref), custom_call_target="tpu_custom_call" | custom-call | tf_op jit(solution)/shard_map/second_kernel/pallas_call | solution.py:317
  82.5 0.1 collective-permute-start.4
  82.6 1.2 %collective-permute-done.4 = f32[8,640]{1,0:T(8,128)S(1)} collective-permute-done((f32[8,640]{1,0:T(8,128)S(1)}, f32[8,640]{1,0:T(8,128)S(1)}, u32[]{:S(2)}, u32[]{:S(2)}) %collective-permute-start.4) | collective-permute-done | bytes 20512 | tf_op jit(solution)/shard_map/ppermute | solution.py:329
  83.8 0.7 collective-permute-start.5
  84.5 4.5 %collective-permute-done.5.far_ref = f32[4,640]{1,0:T(4,128)S(1)} collective-permute-done((f32[4,640]{1,0:T(4,128)S(1)}, f32[4,640]{1,0:T(4,128)S(1)}, u32[]{:S(2)}, u32[]{:S(2)}) %collective-permute-start.5) | collective-permute-done | bytes 10272 | tf_op jit(solution)/shard_map/ppermute | solution.py:329
  89.1 0.4 sums_kernel.1
  89.4 15.9 %all_to_all.16.sums_ref = f32[64,1,128]{2,1,0:T(1,128)S(1)} all-to-all(f32[64,1,128]{2,1,0:T(1,128)S(1)} %get-tuple-element.32), channel_id=1, replica_groups=mesh['blk'=64,'probe'=4] {'blk'}, dimensions={0} | all-to-all | bytes 65536 | tf_op jit(solution)/shard_map/all_to_all | solution.py:333
  105.4 0.8 last_kernel.1
  (4 shorter events, 0.0 us)
Async XLA Ops:
  2.6 35.7 %all-to-all-start = ((bf16[64,48,128]{2,1,0:T(8,128)(2,1)}), bf16[64,48,128]{2,1,0:T(8,128)(2,1)S(1)}, u32[]{:S(2)}, u32[]{:S(2)}) async-start(bf16[64,48,128]{2,1,0:T(8,128)(2,1)} %get-tuple-element.24), calls=%async_computation | async-start | bytes 1572864 | tf_op jit(solution)/shard_map/all_to_all | solution.py:333
  15.3 1.5 %collective-permute-start = (f32[24,160]{1,0:T(8,128)}, f32[24,160]{1,0:T(8,128)S(1)}, u32[]{:S(2)}, u32[]{:S(2)}) collective-permute-start(f32[24,160]{1,0:T(8,128)} %get-tuple-element.21), channel_id=1, source_target_pairs={{0,1},{1,0},{2,3},{3,2},{4,5},{5,4},{6,7},{7,6},{8,9},{9,8},{10,11... | collective-permute-start | bytes 46088 | tf_op jit(solution)/shard_map/ppermute | solution.py:329
  16.8 6.6 %collective-permute-start.1 = (f32[48,160]{1,0:T(8,128)S(1)}, f32[48,160]{1,0:T(8,128)S(1)}, u32[]{:S(2)}, u32[]{:S(2)}) collective-permute-start(f32[48,160]{1,0:T(8,128)S(1)} %constant_dynamic-update-slice_fusion.near_ref), channel_id=1, source_target_pairs={{0,2},{1,3},{2,0},{3,1},{4,6},{5,7},{6,4},{7,5},{8,10},{9,11},{10,... | collective-permute-start | bytes 92168 | tf_op jit(solution)/shard_map/ppermute | solution.py:329
  43.9 1.3 %collective-permute-start.2 = (f32[16,640]{1,0:T(8,128)S(1)}, f32[16,640]{1,0:T(8,128)S(1)}, u32[]{:S(2)}, u32[]{:S(2)}) collective-permute-start(f32[16,640]{1,0:T(8,128)S(1)} %get-tuple-element.25), channel_id=1, source_target_pairs={{0,1},{1,0},{2,3},{3,2},{4,5},{5,4},{6,7},{7,6},{8,9},{9,8},{10,11... | collective-permute-start | bytes 122888 | tf_op jit(solution)/shard_map/ppermute | solution.py:329
  45.2 5.5 %collective-permute-start.3 = (f32[16,640]{1,0:T(8,128)S(1)}, f32[16,640]{1,0:T(8,128)S(1)}, u32[]{:S(2)}, u32[]{:S(2)}) collective-permute-start(f32[16,640]{1,0:T(8,128)S(1)} %add.6.near_ref), channel_id=1, source_target_pairs={{0,2},{1,3},{2,0},{3,1},{4,6},{5,7},{6,4},{7,5},{8,10},{9,11},{10,... | collective-permute-start | bytes 122888 | tf_op jit(solution)/shard_map/ppermute | solution.py:329
  82.5 1.3 %collective-permute-start.4 = (f32[8,640]{1,0:T(8,128)S(1)}, f32[8,640]{1,0:T(8,128)S(1)}, u32[]{:S(2)}, u32[]{:S(2)}) collective-permute-start(f32[8,640]{1,0:T(8,128)S(1)} %get-tuple-element.31), channel_id=1, source_target_pairs={{0,1},{1,0},{2,3},{3,2},{4,5},{5,4},{6,7},{7,6},{8,9},{9,8},{10,11... | collective-permute-start | bytes 61448 | tf_op jit(solution)/shard_map/ppermute | solution.py:329
  83.8 5.3 %collective-permute-start.5 = (f32[4,640]{1,0:T(4,128)S(1)}, f32[4,640]{1,0:T(4,128)S(1)}, u32[]{:S(2)}, u32[]{:S(2)}) collective-permute-start(f32[4,640]{1,0:T(4,128)S(1)} %slice_select_fusion), channel_id=1, source_target_pairs={{0,2},{1,3},{2,0},{3,1},{4,6},{5,7},{6,4},{7,5},{8,10},{9,11},{10,... | collective-permute-start | bytes 30728 | tf_op jit(solution)/shard_map/ppermute | solution.py:329
